TPU v7x, 512 devices: a whole 4x8x8 slice. The times are simulated.
512 devices in a mesh: row: 64 (over y, x, core), col: 8 (over z).
Axes of the slice: x: 4, y: 8, z: 8, core: 2. Of those that a mesh axis runs over, the one named last changes fastest.
Arguments:
- samples: float32 [49152, 8192], P('row', 'col'), may hold values from -6 to 6
- start_basis: float32 [8192, 128], P('col'), may hold values from -6 to 6
Outputs:
- basis: float32 [49152, 128], P('row')
- upper: float32 [128, 128], replicated
- projected: float32 [8, 1024, 128], P('col', 'row')
All inputs are finite; a program needn't handle non-finite values.
Results may differ from a plain program's by a relative error of at most 0.000075.
Values sent between devices are 32-bit elements; how exact they have to be, the bound alone decides.
No kernel may reach another device: no remote copies, remote signals or barrier semaphores. Data moves between devices by JAX's collectives and lax.ppermute only.
A program may use at most 64 MiB of HBM per device.

v0:
```python
import jax
import jax.numpy as jnp
from jax import lax
from jax.sharding import PartitionSpec as P


def solve_rows(lower, values):
    return lax.linalg.triangular_solve(lower, values, left_side=False, lower=True, transpose_a=True)


def inner(left, right):
    return jnp.dot(
        left.T, right, precision=lax.Precision.HIGHEST, preferred_element_type=jnp.float32
    )


def body(samples, start_basis):
    high = lax.Precision.HIGHEST
    total = samples.shape[0] * lax.axis_size("row")
    local = jnp.dot(samples, start_basis, precision=high, preferred_element_type=jnp.float32)
    sketch = lax.psum(local, "col")
    gram = lax.psum(inner(sketch, sketch), "row") / total
    lower = jnp.linalg.cholesky(gram)
    basis = solve_rows(lower, sketch)
    factor = 1.0 / jnp.sqrt(jnp.float32(total))
    share_rows = samples.shape[1] // lax.axis_size("row")
    mine = lax.psum_scatter(inner(samples, basis) * factor, "row", scatter_dimension=0, tiled=True)
    return (basis, lower.T, mine.reshape(1, share_rows, basis.shape[1]))


def solution(mesh):
    in_specs = (P("row", "col"), P("col", None))
    out_specs = (P("row", None), P(), P("col", "row", None))
    return jax.shard_map(body, mesh=mesh, in_specs=in_specs, out_specs=out_specs, check_vma=False)
```

profile of v0, /device:TPU:1, one launch (start us, length us, event | category | flops | bytes accessed | tf_op | source)
XLA Modules:
  0.0 508.5 jit_solution(2737356328046848837)
XLA Ops:
  7.2 0.0 all-reduce.5.cloned.1.call-start
  7.2 1.8 copy-done
  9.1 4.4 fusion.5
  13.4 0.0 all-reduce.5.cloned.1.call-update
  13.5 0.0 all-reduce.7.cloned.1.call-start
  13.5 80.4 %all-reduce.5.cloned.1.call-done = f32[768,128]{1,0:T(8,128)} async-done(((f32[768,128]{1,0:T(8,128)}), f32[768,128]{1,0:T(8,128)}) %all-reduce.5.cloned.1.call-update) | async-done | bytes 393232 | tf_op jit(solution)/shard_map/psum | solution.py:21
  94.0 2.5 fusion.6
  96.5 0.0 all-reduce.7.cloned.1.call-update
  96.5 0.2 all-reduce.9.cloned.1.call-start
  96.8 183.3 %all-reduce.7.cloned.1.call-done = f32[128,128]{0,1:T(8,128)} async-done(((f32[128,128]{0,1:T(8,128)}), f32[128,128]{0,1:T(8,128)}) %all-reduce.7.cloned.1.call-update) | async-done | bytes 65552 | tf_op jit(solution)/shard_map/psum | solution.py:22
  280.1 0.8 broadcast_multiply_fusion
  280.9 0.1 copy.10
  281.0 0.9 fusion.3
  281.9 11.7 %cholesky.16 = f32[128,128]{1,0:T(8,128)S(1)} custom-call(f32[128,128]{1,0:T(8,128)S(1)} %fusion.3), custom_call_target="Cholesky" | custom-call | tf_op jit(solution)/shard_map/jit(cholesky)/cholesky | solution.py:23
  293.6 0.6 compare_reduce_fusion
  294.3 1.3 fusion.4
  295.6 10.4 %custom-call.6 = f32[1,128,128]{1,2,0:T(8,128)} custom-call(f32[1,128,128]{2,1,0:T(8,128)S(1)} %get-tuple-element.10), custom_call_target="InvertDiagBlocksLowerTriangular" | custom-call | tf_op jit(solution)/shard_map/triangular_solve | solution.py:8
  306.0 1.5 fusion.1
  307.5 2.7 fusion
  310.2 1.3 dynamic-slice
  312.1 1.6 copy.11
  313.7 185.2 %all-reduce.9.cloned.1.call-done = f32[1024,128]{0,1:T(8,128)} async-done(((f32[1024,128]{0,1:T(8,128)}), f32[1024,128]{0,1:T(8,128)}) %all-reduce.9.cloned.1.call-update) | async-done | bytes 524304
  498.9 1.5 dynamic-slice_bitcast_fusion
  500.4 1.5 copy.12
  (5 shorter events, 0.1 us)
Async XLA Ops:
  7.2 1.9 copy-start
  7.2 86.8 %all-reduce.5.cloned.1.call-start = ((), (), s32[]{:S(2)}) async-start(), calls=%async_computation | async-start | bytes 786432 | tf_op jit(solution)/shard_map/psum | solution.py:21
  13.5 266.6 %all-reduce.7.cloned.1.call-start = ((), (), s32[]{:S(2)}) async-start(), calls=%async_computation.1 | async-start | bytes 131072 | tf_op jit(solution)/shard_map/psum | solution.py:22
  96.5 402.4 %all-reduce.9.cloned.1.call-start = ((), (), s32[]{:S(2)}) async-start(), calls=%async_computation.2 | async-start | bytes 1048576
  307.5 194.5 %copy-start.1 = (f32[768,128]{1,0:T(8,128)}, f32[768,128]{1,0:T(8,128)S(1)}, u32[]{:S(2)}) copy-start(f32[768,128]{1,0:T(8,128)S(1)} %fusion.1) | copy-start | bytes 1179652
Sparse Core Ops, SparseCore 0:
  13.6 80.3 all-reduce.4
  98.4 181.6 all-reduce.6
  310.3 188.5 all-reduce.8
where the time goes:
time: 509 us; the launch traced here: 508 us
  waiting for transfers between devices  449 us (88%)
  other arithmetic  25.8 us (5%)
  between operations  14.4 us (3%)
  matrix products  11 us (2%)
  local copies, waits for them, and re-layouts  7.83 us (2%)
    unnamed x4, waiting for transfers between devices  185 us
    psum x1, waiting for transfers between devices, body(): gram = lax.psum(inner(sketch, sketch), 'row') / total  183 us
    psum x1, waiting for transfers between devices, body(): sketch = lax.psum(local, 'col')  80.4 us
    another operation x3, other arithmetic, body(): lower = jnp.linalg.cholesky(gram)  12.4 us
    another operation x1, other arithmetic, solve_rows(): lax.linalg.triangular_solve(lower, values, left_side=False, lower=True, t...  10.4 us
  transfers between devices with their start and end apart: 3, of which 3 were waited for; matrix products, arithmetic and copies ran while one was open for 1% of the time, Pallas kernels for 0%

commit v1 on v0

v1 whole, which is shorter than its diff:
```python
import jax
import jax.numpy as jnp
from jax import lax
from jax.sharding import PartitionSpec as P

HIGH = lax.Precision.HIGH
HIGHEST = lax.Precision.HIGHEST


def times(left, right, precision):
    return jnp.dot(left, right, precision=precision, preferred_element_type=jnp.float32)


def exchange(parts, axis):
    return lax.all_to_all(parts, axis, 0, 0)


def body(samples, start_basis):
    rows, columns = samples.shape
    rank = start_basis.shape[1]
    n_row, n_col = lax.axis_size("row"), lax.axis_size("col")
    total = rows * n_row
    share, gram_share = columns // n_row, rank // n_row

    local = times(samples, start_basis, HIGH)
    chunk = exchange(local.reshape(n_col, rows // n_col, rank), "col").sum(0)
    sketch = exchange(jnp.broadcast_to(chunk, (n_col,) + chunk.shape), "col").reshape(rows, rank)

    gram = times(sketch.T, sketch, HIGHEST).reshape(n_row, 1, gram_share, rank)
    wide = times(samples.T, sketch, HIGH).reshape(n_row, share // gram_share, gram_share, rank)
    summed = exchange(jnp.concatenate([wide, gram], axis=1), "row").sum(0)
    mine = summed[:-1].reshape(share, rank)
    gram = exchange(jnp.broadcast_to(summed[-1], (n_row, gram_share, rank)), "row").reshape(rank, rank) / total

    lower = jnp.linalg.cholesky(gram)
    solve = lambda values: lax.linalg.triangular_solve(lower, values, left_side=False, lower=True, transpose_a=True)
    inverse = solve(jnp.eye(rank, dtype=jnp.float32))
    basis = times(sketch, inverse, HIGHEST)
    projected = times(mine, inverse, HIGHEST) * (1.0 / jnp.sqrt(jnp.float32(total)))
    return basis, lower.T, projected.reshape(1, share, rank)


def solution(mesh):
    in_specs = (P("row", "col"), P("col", None))
    out_specs = (P("row", None), P(), P("col", "row", None))
    return jax.shard_map(body, mesh=mesh, in_specs=in_specs, out_specs=out_specs, check_vma=False)
```

time: 509 us -> 145 us (0.28)
  waiting for transfers between devices: 449 us -> 9.4 us
  blocking collectives: 0 us -> 71.3 us
  between operations: 14.4 us -> 0.69 us
  other arithmetic: 25.8 us -> 34.4 us
  starting transfers between devices: 0.3 us -> 5.98 us
    psum x2 -> x0, waiting for transfers between devices: 264 us -> none  [the longest x1 183 us: body(): gram = lax.psum(inner(sketch, sketch), 'row') / total]
    unnamed x4 -> x0, waiting for transfers between devices: 185 us -> none
    all_to_all x0 -> x3, blocking collectives: none -> 71.3 us  [exchange(): return lax.all_to_all(parts, axis, 0, 0)]
    all_to_all x0 -> x1, waiting for transfers between devices: none -> 9.4 us  [exchange(): return lax.all_to_all(parts, axis, 0, 0)]
    all_to_all x0 -> x1, starting transfers between devices: none -> 5.98 us  [exchange(): return lax.all_to_all(parts, axis, 0, 0)]
  transfers between devices with their start and end apart: 3 -> 1, of which waited for: 3 -> 1; matrix products, arithmetic and copies ran while one was open for 1% -> 0% of each run, Pallas kernels for 0% -> 0%
where the time goes in v1:
time: 145 us; the launch traced here: 144 us
  blocking collectives  71.3 us (49%)
  other arithmetic  34.4 us (24%)
  local copies, waits for them, and re-layouts  12.7 us (9%)
  matrix products  9.43 us (7%)
  waiting for transfers between devices  9.4 us (6%)
  starting transfers between devices  5.98 us (4%)
    all_to_all x3, blocking collectives, exchange(): return lax.all_to_all(parts, axis, 0, 0)  71.3 us
    another operation x3, other arithmetic, body(): lower = jnp.linalg.cholesky(gram)  14.7 us
    another operation x1, other arithmetic, body(): lax.linalg.triangular_solve(lower, values, left_side=False, lower=True, t...  11.3 us
    all_to_all x1, waiting for transfers between devices, exchange(): return lax.all_to_all(parts, axis, 0, 0)  9.4 us
    dot_general x5, matrix products, times(): jnp.dot(left, right, precision=precision, preferred_element_type=jnp.floa...  8.41 us
    all_to_all x1, starting transfers between devices, exchange(): return lax.all_to_all(parts, axis, 0, 0)  5.98 us
    dot_general x3, local copies, waits for them, and re-layouts, times(): jnp.dot(left, right, precision=precision, preferred_element_type=jnp.floa...  3.65 us
    unnamed x3, local copies, waits for them, and re-layouts  3.46 us
  transfers between devices with their start and end apart: 1, of which 1 were waited for; matrix products, arithmetic and copies ran while one was open for 0% of the time, Pallas kernels for 0%

profile of v1, /device:TPU:1, one launch (start us, length us, event | category | flops | bytes accessed | tf_op | source)
XLA Modules:
  0.0 143.9 jit_solution(10523349371566747538)
XLA Ops:
  0.6 1.9 %copy-done = f32[768,1024]{1,0:T(8,128)S(1)} copy-done((f32[768,1024]{1,0:T(8,128)S(1)}, f32[768,1024]{1,0:T(8,128)}, u32[]{:S(2)}) %copy-start) | copy-done | bytes 3145752
  2.5 2.4 %fusion.6 = f32[768,128]{1,0:T(8,128)S(1)} fusion(f32[768,1024]{1,0:T(8,128)S(1)} %copy-done, f32[1024,128]{1,0:T(8,128)} %param.3), kind=kOutput, calls=%fused_computation.19 | convolution fusion | flops 603979776 | bytes 4063232 | tf_op jit(solution)/shard_map/dot_general | solution.py:11
  5.0 24.2 %all_to_all.20 = f32[8,96,128]{2,1,0:T(8,128)S(1)} all-to-all(f32[8,96,128]{2,1,0:T(8,128)S(1)} %bitcast.42), channel_id=1, replica_groups=mesh['row'=64,'col'=8] {'col'}, dimensions={0} | all-to-all | bytes 786432 | tf_op jit(solution)/shard_map/all_to_all | solution.py:15
  30.6 14.1 %all_to_all.21 = f32[8,96,128]{2,1,0:T(8,128)S(1)} all-to-all(f32[8,96,128]{2,1,0:T(8,128)S(1)} %broadcast_in_dim.8), channel_id=1, replica_groups=mesh['row'=64,'col'=8] {'col'}, dimensions={0} | all-to-all | bytes 786432 | tf_op jit(solution)/shard_map/all_to_all | solution.py:15
  44.7 0.9 copy.10
  45.7 2.0 %reshape.43 = f32[64,2,768]{2,1,0:T(2,128)} reshape(f32[128,768]{1,0:T(8,128)} %copy.10) | data formatting | bytes 786432 | tf_op jit(solution)/shard_map/reshape.16
  47.6 1.5 %convolution_bitcast_fusion.1 = f32[64,1,2,128]{3,0,2,1:T(8,128)S(1)} fusion(f32[768,128,1]{1,0,2:T(8,128)S(1)} %bitcast.38, f32[64,2,768]{2,1,0:T(2,128)} %reshape.43), kind=kOutput, calls=%fused_computation.1 | convolution fusion | flops 150994944 | bytes 851968 | tf_op jit(solution)/shard_map/dot_general | solution.py:11
  49.8 1.8 %convolution_bitcast_fusion = f32[1024,128]{0,1:T(8,128)} fusion(f32[768,128]{1,0:T(8,128)S(1)} %bitcast.39, f32[768,1024]{1,0:T(8,128)S(1)} %copy-done), kind=kOutput, calls=%fused_computation | convolution fusion | flops 603979776 | bytes 4063232 | tf_op jit(solution)/shard_map/dot_general | solution.py:11
  51.6 2.1 %copy.9 = f32[1024,128]{1,0:T(8,128)} copy(f32[1024,128]{0,1:T(8,128)} %convolution_bitcast_fusion) | data formatting | bytes 1048576 | tf_op jit(solution)/shard_map/dot_general | solution.py:11
  53.7 1.3 pad_maximum_fusion
  55.0 33.0 %all_to_all.22 = f32[64,9,2,128]{3,2,1,0:T(2,128)} all-to-all(f32[64,9,2,128]{3,2,1,0:T(2,128)S(1)} %pad_maximum_fusion), channel_id=1, replica_groups=mesh['row'=64,'col'=8] {'row'}, dimensions={0} | all-to-all | bytes 1179648 | tf_op jit(solution)/shard_map/all_to_all | solution.py:15
  88.0 1.3 reduce_sum.19
  90.0 6.0 %all-to-all-start.3 = ((f32[64,2,128]{2,1,0:T(2,128)}), f32[64,2,128]{2,1,0:T(2,128)}, u32[]{:S(2)}, u32[]{:S(2)}) async-start(f32[64,2,128]{2,1,0:T(2,128)} %broadcast_in_dim.9), calls=%async_computation.3 | async-start | bytes 131072 | tf_op jit(solution)/shard_map/all_to_all | solution.py:15
  96.5 9.4 %all-to-all-done.3 = f32[64,2,128]{2,1,0:T(2,128)} async-done(((f32[64,2,128]{2,1,0:T(2,128)}), f32[64,2,128]{2,1,0:T(2,128)}, u32[]{:S(2)}, u32[]{:S(2)}) %all-to-all-start.3) | async-done | bytes 65568 | tf_op jit(solution)/shard_map/all_to_all | solution.py:15
  105.9 1.5 %broadcast_multiply_fusion = f32[64,2,128]{2,1,0:T(2,128)} fusion(f32[64,2,128]{2,1,0:T(2,128)} %all-to-all-done.3), kind=kLoop, calls=%fused_computation.16 | loop fusion | flops 16384 | bytes 131072 | tf_op jit(solution)/shard_map/div | solution.py:33
  107.4 1.6 %copy.13 = f32[128,128]{0,1:T(8,128)} copy(f32[128,128]{1,0:T(8,128)} %bitcast.43) | data formatting | bytes 131072 | tf_op jit(solution)/shard_map/div | solution.py:33
  109.0 1.5 %fusion.4 = f32[128,128]{1,0:T(8,128)} fusion(f32[128,128]{1,0:T(8,128)} %bitcast.44, f32[128,128]{0,1:T(8,128)} %copy.13), kind=kLoop, calls=%fused_computation.9 | loop fusion | flops 32768 | bytes 196608 | tf_op jit(solution)/shard_map/jit(cholesky)/div | solution.py:35
  110.5 13.2 %cholesky.14 = f32[128,128]{1,0:T(8,128)} custom-call(f32[128,128]{1,0:T(8,128)} %fusion.4), custom_call_target="Cholesky" | custom-call | tf_op jit(solution)/shard_map/jit(cholesky)/cholesky | solution.py:35
  125.2 2.1 %fusion.5 = (f32[128,128]{0,1:T(8,128)}, f32[1,128,128]{2,1,0:T(8,128)}) fusion(f32[128,128]{1,0:T(8,128)} %cholesky.14, pred[]{:T(512)} %compare_reduce_fusion), kind=kLoop, calls=%fused_computation.15 | loop fusion | flops 65536 | bytes 196609 | tf_op jit(solution)/shard_map/transpose | solution.py:40
  127.4 1.6 %copy.14 = f32[128,128]{1,0:T(8,128)} copy(f32[128,128]{0,1:T(8,128)} %get-tuple-element.9) | data formatting | bytes 131072
  128.9 11.3 %custom-call.6 = f32[1,128,128]{1,2,0:T(8,128)} custom-call(f32[1,128,128]{2,1,0:T(8,128)} %get-tuple-element.10), custom_call_target="InvertDiagBlocksLowerTriangular" | custom-call | tf_op jit(solution)/shard_map/triangular_solve | solution.py:36
  140.2 1.0 fusion.2
  141.2 1.2 fusion.7
  142.4 1.5 %fusion = f32[1,16,128]{2,1,0:T(8,128)} fusion(f32[16,128]{1,0:T(8,128)} %bitcast.45, f32[128,128]{1,0:T(8,128)S(1)} %fusion.2), kind=kOutput, calls=%fused_computation.3 | convolution fusion | flops 3147776 | bytes 81920 | tf_op jit(solution)/shard_map/dot_general | solution.py:11
  (9 shorter events, 4.9 us)
Async XLA Ops:
  0.6 1.9 %copy-start = (f32[768,1024]{1,0:T(8,128)S(1)}, f32[768,1024]{1,0:T(8,128)}, u32[]{:S(2)}) copy-start(f32[768,1024]{1,0:T(8,128)} %param.2) | copy-start | bytes 9437188
  90.0 16.0 %all-to-all-start.3 = ((f32[64,2,128]{2,1,0:T(2,128)}), f32[64,2,128]{2,1,0:T(2,128)}, u32[]{:S(2)}, u32[]{:S(2)}) async-start(f32[64,2,128]{2,1,0:T(2,128)} %broadcast_in_dim.9), calls=%async_computation.3 | async-start | bytes 131072 | tf_op jit(solution)/shard_map/all_to_all | solution.py:15

commit v2 on v1

v2 whole, which is shorter than its diff:
```python
import functools

import jax
import jax.numpy as jnp
from jax import lax
from jax.experimental import pallas as pl
from jax.experimental.pallas import tpu as pltpu
from jax.sharding import PartitionSpec as P

F32, BF16 = jnp.float32, jnp.bfloat16
HIGHEST = lax.Precision.HIGHEST
WHOLE = pl.BlockSpec(memory_space=pltpu.VMEM)
SUBLANES = 8


def halves(values):
    high = values.astype(BF16)
    return high, (values - high.astype(F32)).astype(BF16)


def dot(left, right, axes, precision=None):
    return lax.dot_general(
        left, right, (axes, ((), ())), precision=precision, preferred_element_type=F32
    )


def cost(flops, read, written):
    return pl.CostEstimate(flops=flops, bytes_accessed=4 * (read + written), transcendentals=0)


def split_dot(left, right_halves, axes):
    high, low = halves(left)
    both = dot(high, right_halves, axes) + dot(low, right_halves, axes)
    rank = right_halves.shape[1] // 2
    return both[:, :rank] + both[:, rank:]


def sketch_kernel(samples_ref, start_ref, local_ref, start_halves):
    @pl.when(pl.program_id(0) == 0)
    def _():
        high, low = halves(start_ref[...])
        rank = high.shape[1]
        start_halves[:, :rank] = high
        start_halves[:, rank:] = low

    local_ref[...] = split_dot(samples_ref[...], start_halves[...], ((1,), (0,)))


def sketch_product(samples, start_basis, step=128):
    rows, columns = samples.shape
    rank = start_basis.shape[1]
    return pl.pallas_call(
        sketch_kernel,
        grid=(rows // step,),
        in_specs=[
            pl.BlockSpec((step, columns), lambda i: (i, 0)),
            pl.BlockSpec((columns, rank), lambda i: (0, 0)),
        ],
        out_specs=pl.BlockSpec((step, rank), lambda i: (i, 0)),
        out_shape=jax.ShapeDtypeStruct((rows, rank), F32),
        scratch_shapes=[pltpu.VMEM((columns, 2 * rank), BF16)],
        cost_estimate=cost(8 * rows * columns * rank, rows * columns, rows * rank),
        name="sketch_product",
    )(samples, start_basis)


def sum_kernel(parts_ref, out_ref):
    total = parts_ref[0]
    for i in range(1, parts_ref.shape[0]):
        total = total + parts_ref[i]
    for i in range(out_ref.shape[0]):
        out_ref[i] = total


def sum_and_copy(parts):
    return pl.pallas_call(
        sum_kernel,
        in_specs=[WHOLE],
        out_specs=WHOLE,
        out_shape=jax.ShapeDtypeStruct(parts.shape, F32),
        cost_estimate=cost(parts.size, parts.size, parts.size),
        name="sum_and_copy",
    )(parts)


def gram_kernel(sketch_ref, gram_ref):
    sketch = sketch_ref[...]
    gram_ref[...] = dot(sketch, sketch, ((0,), (0,)), HIGHEST)


def gram_product(sketch):
    rows, rank = sketch.shape
    return pl.pallas_call(
        gram_kernel,
        in_specs=[WHOLE],
        out_specs=WHOLE,
        out_shape=jax.ShapeDtypeStruct((rank, rank), F32),
        cost_estimate=cost(2 * rows * rank * rank, rows * rank, rank * rank),
        name="gram_product",
    )(sketch)


def gram_sum_kernel(share, parts_ref, out_ref):
    rows = parts_ref.shape[0]
    total = parts_ref[:SUBLANES]
    for at in range(SUBLANES, rows, SUBLANES):
        total = total + parts_ref[at : at + SUBLANES]
    mine = total[:share]
    for at in range(share, SUBLANES, share):
        mine = mine + total[at : at + share]
    tile = jnp.concatenate([mine] * (SUBLANES // share), axis=0)
    for at in range(0, rows, SUBLANES):
        out_ref[at : at + SUBLANES] = tile


def gram_sum(parts, share):
    return pl.pallas_call(
        functools.partial(gram_sum_kernel, share),
        in_specs=[WHOLE],
        out_specs=WHOLE,
        out_shape=jax.ShapeDtypeStruct(parts.shape, F32),
        cost_estimate=cost(parts.size, parts.size, parts.size),
        name="gram_sum",
    )(parts)


def wide_kernel(samples_ref, sketch_ref, wide_ref, sketch_halves):
    @pl.when(pl.program_id(0) == 0)
    def _():
        high, low = halves(sketch_ref[...])
        rank = high.shape[1]
        sketch_halves[:, :rank] = high
        sketch_halves[:, rank:] = low

    wide_ref[...] = split_dot(samples_ref[...], sketch_halves[...], ((0,), (0,)))


def wide_product(samples, sketch, step=256):
    rows, columns = samples.shape
    rank = sketch.shape[1]
    return pl.pallas_call(
        wide_kernel,
        grid=(columns // step,),
        in_specs=[
            pl.BlockSpec((rows, step), lambda i: (0, i)),
            pl.BlockSpec((rows, rank), lambda i: (0, 0)),
        ],
        out_specs=pl.BlockSpec((step, rank), lambda i: (i, 0)),
        out_shape=jax.ShapeDtypeStruct((columns, rank), F32),
        scratch_shapes=[pltpu.VMEM((rows, 2 * rank), BF16)],
        cost_estimate=cost(8 * rows * columns * rank, rows * columns, columns * rank),
        name="wide_product",
    )(samples, sketch)


def factor_kernel(scale, gram_ref, sketch_ref, basis_ref, upper_ref, inverse_ref):
    size = gram_ref.shape[0]
    count = size // SUBLANES
    lane = lax.broadcasted_iota(jnp.int32, (SUBLANES, size), 1)
    sub = lax.broadcasted_iota(jnp.int32, (SUBLANES, size), 0)
    down = lambda values, row: jnp.broadcast_to(values[row : row + 1, :], values.shape)
    across = lambda values, column: jnp.broadcast_to(values[:, column : column + 1], values.shape)
    tiles = [gram_ref[SUBLANES * t : SUBLANES * (t + 1), :] * scale for t in range(count)]
    for j in range(count):
        base = SUBLANES * j
        inside = (lane >= base) & (lane < base + SUBLANES)
        rest = range(j + 1, count)
        own = [across(tiles[j], base + k) for k in range(SUBLANES)]
        below = {t: [across(tiles[t], base + k) for k in range(SUBLANES)] for t in rest}
        panel = jnp.where(inside, jnp.where(lane - base == sub, 1.0, 0.0), tiles[j])
        for t in rest:
            tiles[t] = jnp.where(inside, 0.0, tiles[t])
        diagonal = jnp.ones_like(panel)
        for k in range(SUBLANES):
            pivot = down(own[k], k)
            diagonal = jnp.where(sub == k, pivot, diagonal)
            reciprocal = 1.0 / pivot
            heads = {i: down(own[i], k) for i in range(k + 1, SUBLANES)}
            row = down(panel, k)
            factor = jnp.where(sub > k, own[k] * reciprocal, 0.0)
            for i in heads:
                own[i] = own[i] - factor * heads[i]
            panel = panel - factor * row
            for t in rest:
                factor = below[t][k] * reciprocal
                for i in heads:
                    below[t][i] = below[t][i] - factor * heads[i]
                tiles[t] = tiles[t] - factor * row
        root = lax.rsqrt(diagonal)
        done = panel * root
        block = jnp.zeros_like(panel)
        for k in range(SUBLANES):
            block = jnp.where(lane == base + k, own[k] * root, block)
        block = jnp.where(lane - base >= sub, block, 0.0)
        here = slice(base, base + SUBLANES)
        upper_ref[here, :] = jnp.where(lane >= base + SUBLANES, done, block)
        inverse_ref[here, :] = jnp.where(lane < base + SUBLANES, done, 0.0)
    basis_ref[...] = dot(sketch_ref[...], inverse_ref[...], ((1,), (1,)), HIGHEST)


def factor(gram, sketch, scale):
    rows, rank = sketch.shape
    square = jax.ShapeDtypeStruct(gram.shape, F32)
    return pl.pallas_call(
        functools.partial(factor_kernel, scale),
        in_specs=[WHOLE, WHOLE],
        out_specs=(WHOLE,) * 3,
        out_shape=(jax.ShapeDtypeStruct(sketch.shape, F32), square, square),
        cost_estimate=cost(50 * 2 * rows * rank * rank, rows * rank, rows * rank),
        name="factor",
    )(gram, sketch)


def project_kernel(scale, parts_ref, inverse_ref, out_ref):
    total = parts_ref[0]
    for i in range(1, parts_ref.shape[0]):
        total = total + parts_ref[i]
    out_ref[0] = dot(total, inverse_ref[...], ((1,), (1,)), HIGHEST) * scale


def project(parts, inverse, scale):
    return pl.pallas_call(
        functools.partial(project_kernel, scale),
        in_specs=[WHOLE, WHOLE],
        out_specs=WHOLE,
        out_shape=jax.ShapeDtypeStruct((1,) + parts.shape[1:], F32),
        cost_estimate=cost(parts.size, parts.size, inverse.size),
        name="project",
    )(parts, inverse)


def exchange(parts, axis):
    return lax.all_to_all(parts, axis, 0, 0)


def body(samples, start_basis):
    rows, columns = samples.shape
    rank = start_basis.shape[1]
    n_row, n_col = lax.axis_size("row"), lax.axis_size("col")
    total = rows * n_row
    share, gram_share = columns // n_row, rank // n_row

    local = sketch_product(samples, start_basis)
    chunks = sum_and_copy(exchange(local.reshape(n_col, rows // n_col, rank), "col"))
    sketch = exchange(chunks, "col").reshape(rows, rank)

    gram = exchange(gram_product(sketch).reshape(n_row, gram_share, rank), "row")
    wide = wide_product(samples, sketch).reshape(n_row, share, rank)
    gram = gram_sum(gram.reshape(rank, rank), gram_share)
    gram = exchange(gram.reshape(n_row, gram_share, rank), "row").reshape(rank, rank)
    wide = exchange(wide, "row")
    basis, upper, inverse = factor(gram, sketch, 1.0 / total)
    return basis, upper, project(wide, inverse, 1.0 / total**0.5)


def solution(mesh):
    in_specs = (P("row", "col"), P("col", None))
    out_specs = (P("row", None), P(), P("col", "row", None))
    return jax.shard_map(body, mesh=mesh, in_specs=in_specs, out_specs=out_specs, check_vma=False)
```

time: 145 us -> 117 us (0.81)
  other arithmetic: 34.4 us -> 0 us
  Pallas kernels: 0 us -> 24.1 us
  local copies, waits for them, and re-layouts: 12.7 us -> 0.8 us
  matrix products: 9.43 us -> 0 us
  waiting for transfers between devices: 9.4 us -> 16.8 us
  blocking collectives: 71.3 us -> 64.5 us
  starting transfers between devices: 5.98 us -> 9.38 us
    another operation x4 -> x0, other arithmetic: 26 us -> none  [the longest x3 14.7 us: body(): lower = jnp.linalg.cholesky(gram)]
    pallas_call x0 -> x7, Pallas kernels: none -> 24.1 us  [the longest x1 6.36 us: factor(): pl.pallas_call(functools.partial(factor_kernel, scale), in_specs=[WHOLE,...]
    dot_general x5 -> x0, matrix products: 8.41 us -> none  [times(): jnp.dot(left, right, precision=precision, preferred_element_type=jnp.floa...]
    all_to_all x1 -> x2, waiting for transfers between devices: 9.4 us -> 16.8 us  [exchange(): return lax.all_to_all(parts, axis, 0, 0)]
    all_to_all x3, blocking collectives: 71.3 us -> 64.5 us  [exchange(): return lax.all_to_all(parts, axis, 0, 0)]
    dot_general x3 -> x0, local copies, waits for them, and re-layouts: 3.65 us -> none  [times(): jnp.dot(left, right, precision=precision, preferred_element_type=jnp.floa...]
    all_to_all x1 -> x2, starting transfers between devices: 5.98 us -> 9.38 us  [exchange(): return lax.all_to_all(parts, axis, 0, 0)]
    div x2 -> x0, other arithmetic: 3.01 us -> none  [the longest x1 1.51 us: body(): lower = jnp.linalg.cholesky(gram)]
  transfers between devices with their start and end apart: 1 -> 2, of which waited for: 1 -> 2; matrix products, arithmetic and copies ran while one was open for 0% -> 0% of each run, Pallas kernels for 0% -> 9%
where the time goes in v2:
time: 117 us; the launch traced here: 116 us
  blocking collectives  64.5 us (55%)
  Pallas kernels  24.1 us (21%)
  waiting for transfers between devices  16.8 us (14%)
  starting transfers between devices  9.38 us (8%)
    all_to_all x3, blocking collectives, exchange(): return lax.all_to_all(parts, axis, 0, 0)  64.5 us
    all_to_all x2, waiting for transfers between devices, exchange(): return lax.all_to_all(parts, axis, 0, 0)  16.8 us
    all_to_all x2, starting transfers between devices, exchange(): return lax.all_to_all(parts, axis, 0, 0)  9.38 us
    pallas_call x1, Pallas kernels, factor(): pl.pallas_call(functools.partial(factor_kernel, scale), in_specs=[WHOLE,...  6.36 us
    pallas_call x1, Pallas kernels, sketch_product(): pl.pallas_call(sketch_kernel, grid=(rows // step,), in_specs=[pl.BlockSpe...  5.74 us
    pallas_call x1, Pallas kernels, wide_product(): pl.pallas_call(wide_kernel, grid=(columns // step,), in_specs=[pl.BlockSp...  4.66 us
  transfers between devices with their start and end apart: 2, of which 2 were waited for; matrix products, arithmetic and copies ran while one was open for 0% of the time, Pallas kernels for 9%

profile of v2, /device:TPU:1, one launch (start us, length us, event | category | flops | bytes accessed | tf_op | source)
XLA Modules:
  0.0 116.2 jit_solution(15523957432782705298)
XLA Ops:
  0.6 5.7 %sketch_product.1 = f32[768,128]{1,0:T(8,128)} custom-call(f32[768,1024]{1,0:T(8,128)} %samples_ref.3, f32[1024,128]{1,0:T(8,128)} %start_ref.1), custom_call_target="tpu_custom_call" | custom-call | flops 805306368 | bytes 3538944 | tf_op jit(solution)/shard_map/sketch_product/pallas_call | solution.py:52
  6.4 24.5 %all_to_all.25.parts_ref = f32[8,96,128]{2,1,0:T(8,128)} all-to-all(f32[8,96,128]{2,1,0:T(8,128)} %bitcast.11), channel_id=1, replica_groups=mesh['row'=64,'col'=8] {'col'}, dimensions={0} | all-to-all | bytes 786432 | tf_op jit(solution)/shard_map/all_to_all | solution.py:233
  30.8 1.8 %sum_and_copy.1 = f32[8,96,128]{2,1,0:T(8,128)} custom-call(f32[8,96,128]{2,1,0:T(8,128)} %all_to_all.25.parts_ref), custom_call_target="tpu_custom_call" | custom-call | flops 98304 | bytes 786432 | tf_op jit(solution)/shard_map/sum_and_copy/pallas_call | solution.py:76
  32.6 15.8 %all_to_all.26 = f32[8,96,128]{2,1,0:T(8,128)} all-to-all(f32[8,96,128]{2,1,0:T(8,128)} %sum_and_copy.1), channel_id=1, replica_groups=mesh['row'=64,'col'=8] {'col'}, dimensions={0} | all-to-all | bytes 786432 | tf_op jit(solution)/shard_map/all_to_all | solution.py:233
  48.4 2.2 %gram_product.1 = f32[128,128]{1,0:T(8,128)} custom-call(f32[768,128]{1,0:T(8,128)} %bitcast.7), custom_call_target="tpu_custom_call" | custom-call | flops 25165824 | bytes 458752 | tf_op jit(solution)/shard_map/gram_product/pallas_call | solution.py:93
  50.6 24.2 %all_to_all.27 = f32[64,2,128]{2,1,0:T(2,128)} all-to-all(f32[64,2,128]{2,1,0:T(2,128)} %bitcast.12), channel_id=1, replica_groups=mesh['row'=64,'col'=8] {'row'}, dimensions={0} | all-to-all | bytes 131072 | tf_op jit(solution)/shard_map/all_to_all | solution.py:233
  74.8 1.5 %gram_sum.1 = f32[128,128]{1,0:T(8,128)} custom-call(f32[128,128]{1,0:T(8,128)} %bitcast.14), custom_call_target="tpu_custom_call" | custom-call | flops 16384 | bytes 131072 | tf_op jit(solution)/shard_map/gram_sum/pallas_call | solution.py:117
  76.3 4.4 %all-to-all-start.3 = ((f32[64,2,128]{2,1,0:T(2,128)}), f32[64,2,128]{2,1,0:T(2,128)S(1)}, u32[]{:S(2)}, u32[]{:S(2)}) async-start(f32[64,2,128]{2,1,0:T(2,128)} %bitcast.13), calls=%async_computation.3 | async-start | bytes 131072 | tf_op jit(solution)/shard_map/all_to_all | solution.py:233
  80.7 4.7 %wide_product.1 = f32[1024,128]{1,0:T(8,128)} custom-call(f32[768,1024]{1,0:T(8,128)} %samples_ref.3, f32[768,128]{1,0:T(8,128)} %bitcast.8), custom_call_target="tpu_custom_call" | custom-call | flops 805306368 | bytes 3670016 | tf_op jit(solution)/shard_map/wide_product/pallas_call | solution.py:141
  85.4 5.5 %all-to-all-done.3 = f32[64,2,128]{2,1,0:T(2,128)S(1)} async-done(((f32[64,2,128]{2,1,0:T(2,128)}), f32[64,2,128]{2,1,0:T(2,128)S(1)}, u32[]{:S(2)}, u32[]{:S(2)}) %all-to-all-start.3) | async-done | bytes 65568 | tf_op jit(solution)/shard_map/all_to_all | solution.py:233
  90.8 0.0 copy-start.1
  90.9 4.9 %all-to-all-start.4 = ((f32[64,16,128]{2,1,0:T(8,128)}), f32[64,16,128]{2,1,0:T(8,128)S(1)}, u32[]{:S(2)}, u32[]{:S(2)}) async-start(f32[64,16,128]{2,1,0:T(8,128)} %bitcast.10), calls=%async_computation.4 | async-start | bytes 1048576 | tf_op jit(solution)/shard_map/all_to_all | solution.py:233
  95.8 0.0 copy-done.1
  95.8 6.4 %factor.1 = (f32[768,128]{1,0:T(8,128)}, f32[128,128]{1,0:T(8,128)}, f32[128,128]{1,0:T(8,128)}) custom-call(f32[128,128]{1,0:T(8,128)} %bitcast.15, f32[768,128]{1,0:T(8,128)} %bitcast.9), custom_call_target="tpu_custom_call" | custom-call | flops 1258291200 | bytes 786432 | tf_op jit(solution)/shard_map/factor/pallas_call | solution.py:204
  102.2 11.3 %all-to-all-done.4.parts_ref = f32[64,16,128]{2,1,0:T(8,128)S(1)} async-done(((f32[64,16,128]{2,1,0:T(8,128)}), f32[64,16,128]{2,1,0:T(8,128)S(1)}, u32[]{:S(2)}, u32[]{:S(2)}) %all-to-all-start.4) | async-done | bytes 524320 | tf_op jit(solution)/shard_map/all_to_all | solution.py:233
  113.5 0.0 copy-start
  113.5 0.8 copy-done
  114.3 1.9 %project.1 = f32[1,16,128]{2,1,0:T(8,128)} custom-call(f32[64,16,128]{2,1,0:T(8,128)} %copy-done, f32[128,128]{1,0:T(8,128)} %get-tuple-element.8.inverse_ref), custom_call_target="tpu_custom_call" | custom-call | flops 131072 | bytes 589824 | tf_op jit(solution)/shard_map/project/pallas_call | solution.py:222
Async XLA Ops:
  76.3 14.6 %all-to-all-start.3 = ((f32[64,2,128]{2,1,0:T(2,128)}), f32[64,2,128]{2,1,0:T(2,128)S(1)}, u32[]{:S(2)}, u32[]{:S(2)}) async-start(f32[64,2,128]{2,1,0:T(2,128)} %bitcast.13), calls=%async_computation.3 | async-start | bytes 131072 | tf_op jit(solution)/shard_map/all_to_all | solution.py:233
  90.8 5.0 %copy-start.1 = (f32[64,2,128]{2,1,0:T(2,128)}, f32[64,2,128]{2,1,0:T(2,128)S(1)}, u32[]{:S(2)}) copy-start(f32[64,2,128]{2,1,0:T(2,128)S(1)} %all-to-all-done.3) | copy-start | bytes 196612
  90.9 22.7 %all-to-all-start.4 = ((f32[64,16,128]{2,1,0:T(8,128)}), f32[64,16,128]{2,1,0:T(8,128)S(1)}, u32[]{:S(2)}, u32[]{:S(2)}) async-start(f32[64,16,128]{2,1,0:T(8,128)} %bitcast.10), calls=%async_computation.4 | async-start | bytes 1048576 | tf_op jit(solution)/shard_map/all_to_all | solution.py:233
  113.5 0.8 copy-start

commit v3 on v2

v3 whole, which is shorter than its diff:
```python
import functools

import jax
import jax.numpy as jnp
from jax import lax
from jax.experimental import pallas as pl
from jax.experimental.pallas import tpu as pltpu
from jax.sharding import PartitionSpec as P

F32, BF16 = jnp.float32, jnp.bfloat16
HIGHEST = lax.Precision.HIGHEST
WHOLE = pl.BlockSpec(memory_space=pltpu.VMEM)
SUBLANES = 8
LIMIT = 12 * 2**20


def halves(values):
    high = values.astype(BF16)
    return high, (values - high.astype(F32)).astype(BF16)


def dot(left, right, axes, precision=None):
    return lax.dot_general(
        left, right, (axes, ((), ())), precision=precision, preferred_element_type=F32
    )


def cost(flops, read, written):
    return pl.CostEstimate(flops=flops, bytes_accessed=4 * (read + written), transcendentals=0)


def split_dot(left, right_halves, axes):
    high, low = halves(left)
    both = dot(high, right_halves, axes) + dot(low, right_halves, axes)
    rank = right_halves.shape[1] // 2
    return both[:, :rank] + both[:, rank:]


def sketch_kernel(step, samples_ref, start_ref, local_ref, held_ref, start, start_halves, sems, start_sem):
    rows = local_ref.shape[0]
    rank = local_ref.shape[1]
    first = pltpu.make_async_copy(start_ref, start, start_sem)
    first.start()
    copies = []
    for i in range(rows // step):
        at = pl.ds(i * step, step)
        copies.append(pltpu.make_async_copy(samples_ref.at[at], held_ref.at[at], sems.at[i]))
        copies[-1].start()
    first.wait()
    high, low = halves(start[...])
    start_halves[:, :rank] = high
    start_halves[:, rank:] = low
    for i, copy in enumerate(copies):
        copy.wait()
        at = pl.ds(i * step, step)
        local_ref[at] = split_dot(held_ref[at], start_halves[...], ((1,), (0,)))


def sketch_product(samples, start_basis, step=128):
    rows, columns = samples.shape
    rank = start_basis.shape[1]
    return pl.pallas_call(
        functools.partial(sketch_kernel, step),
        in_specs=[pl.BlockSpec(memory_space=pltpu.HBM)] * 2,
        out_specs=(WHOLE, WHOLE),
        out_shape=(
            jax.ShapeDtypeStruct((rows, rank), F32),
            jax.ShapeDtypeStruct((rows, columns), F32),
        ),
        scratch_shapes=[
            pltpu.VMEM((columns, rank), F32),
            pltpu.VMEM((columns, 2 * rank), BF16),
            pltpu.SemaphoreType.DMA((rows // step,)),
            pltpu.SemaphoreType.DMA,
        ],
        compiler_params=pltpu.CompilerParams(vmem_limit_bytes=LIMIT),
        cost_estimate=cost(8 * rows * columns * rank, rows * columns, rows * rank),
        name="sketch_product",
    )(samples, start_basis)


def sum_kernel(parts_ref, out_ref):
    total = parts_ref[0]
    for i in range(1, parts_ref.shape[0]):
        total = total + parts_ref[i]
    for i in range(out_ref.shape[0]):
        out_ref[i] = total


def sum_and_copy(parts):
    return pl.pallas_call(
        sum_kernel,
        in_specs=[WHOLE],
        out_specs=WHOLE,
        out_shape=jax.ShapeDtypeStruct(parts.shape, F32),
        compiler_params=pltpu.CompilerParams(vmem_limit_bytes=LIMIT),
        cost_estimate=cost(parts.size, parts.size, parts.size),
        name="sum_and_copy",
    )(parts)


def gram_kernel(share, sketch_ref, out_ref):
    sketch = sketch_ref[...]
    gram = dot(sketch, sketch, ((0,), (0,)), HIGHEST)
    for at in range(0, gram.shape[0], share):
        part = gram[at : at + share]
        out_ref[2 * at : 2 * at + 2 * share] = jnp.concatenate([part, part], axis=0)


def gram_product(sketch, share):
    rows, rank = sketch.shape
    return pl.pallas_call(
        functools.partial(gram_kernel, share),
        in_specs=[WHOLE],
        out_specs=WHOLE,
        out_shape=jax.ShapeDtypeStruct((2 * rank, rank), F32),
        compiler_params=pltpu.CompilerParams(vmem_limit_bytes=LIMIT),
        cost_estimate=cost(2 * rows * rank * rank, rows * rank, rank * rank),
        name="gram_product",
    )(sketch)


def wide_kernel(step, share, samples_ref, sketch_ref, own_ref, other_ref, sketch_halves):
    core = lax.axis_index("core")
    rank = sketch_ref.shape[1]
    high, low = halves(sketch_ref[...])
    sketch_halves[:, :rank] = high
    sketch_halves[:, rank:] = low
    for at in range(0, samples_ref.shape[1], step):
        wide = split_dot(samples_ref[:, at : at + step], sketch_halves[...], ((0,), (0,)))
        for chip in range(step // (2 * share)):
            pair = [wide[share * (2 * chip + i) : share * (2 * chip + i + 1)] for i in range(2)]
            here = slice(at // 2 + share * chip, at // 2 + share * (chip + 1))
            own_ref[here] = jnp.where(core == 0, pair[0], pair[1])
            other_ref[here] = jnp.where(core == 0, pair[1], pair[0])


def wide_product(samples, sketch, share, step=256):
    rows, columns = samples.shape
    rank = sketch.shape[1]
    half = jax.ShapeDtypeStruct((columns // 2, rank), F32)
    return pl.pallas_call(
        functools.partial(wide_kernel, step, share),
        in_specs=[WHOLE, WHOLE],
        out_specs=(WHOLE, WHOLE),
        out_shape=(half, half),
        scratch_shapes=[pltpu.VMEM((rows, 2 * rank), BF16)],
        compiler_params=pltpu.CompilerParams(vmem_limit_bytes=LIMIT),
        cost_estimate=cost(8 * rows * columns * rank, rows * columns, columns * rank),
        name="wide_product",
    )(samples, sketch)


def turned(values):
    return jnp.concatenate([values[4:], values[:4]], axis=0)


def pack_kernel(parts_ref, own_ref, received_ref, out_ref):
    tile = parts_ref[:SUBLANES]
    for at in range(SUBLANES, parts_ref.shape[0], SUBLANES):
        tile = tile + parts_ref[at : at + SUBLANES]
    gram = tile[:4] + tile[4:]
    gram = jnp.concatenate([gram, gram], axis=0)
    first = lax.broadcasted_iota(jnp.int32, gram.shape, 0) < 4
    for pair in range(out_ref.shape[0] // 40):
        rows = [slice(32 * pair + 8 * i, 32 * pair + 8 * i + 8) for i in range(4)]
        a, b, c, d = [own_ref[here] + received_ref[here] for here in rows]
        c, d = turned(c), turned(d)
        tiles = (a, b, jnp.where(first, gram, c), jnp.where(first, c, d), jnp.where(first, d, gram))
        for i, value in enumerate(tiles):
            out_ref[40 * pair + 8 * i : 40 * pair + 8 * i + 8] = value


def pack(parts, own, received):
    rows = own.shape[0] // 16 * 20
    return pl.pallas_call(
        pack_kernel,
        in_specs=[WHOLE] * 3,
        out_specs=WHOLE,
        out_shape=jax.ShapeDtypeStruct((rows, own.shape[1]), F32),
        compiler_params=pltpu.CompilerParams(vmem_limit_bytes=LIMIT),
        cost_estimate=cost(parts.size, parts.size, rows * 128),
        name="pack",
    )(parts, own, received)


def factor_kernel(total, parts_ref, sketch_ref, basis_ref, upper_ref, projected_ref, inverse_ref):
    size = upper_ref.shape[0]
    count = size // SUBLANES
    lane = lax.broadcasted_iota(jnp.int32, (SUBLANES, size), 1)
    sub = lax.broadcasted_iota(jnp.int32, (SUBLANES, size), 0)
    down = lambda values, row: jnp.broadcast_to(values[row : row + 1, :], values.shape)
    across = lambda values, column: jnp.broadcast_to(values[:, column : column + 1], values.shape)
    half = sub < 4
    piece = lambda at: parts_ref[at : at + SUBLANES]
    tiles = [jnp.where(half, piece(40 * t + 16), piece(40 * t + 32)) / total for t in range(count)]
    for j in range(count):
        base = SUBLANES * j
        inside = (lane >= base) & (lane < base + SUBLANES)
        rest = range(j + 1, count)
        own = [across(tiles[j], base + k) for k in range(SUBLANES)]
        below = {t: [across(tiles[t], base + k) for k in range(SUBLANES)] for t in rest}
        panel = jnp.where(inside, jnp.where(lane - base == sub, 1.0, 0.0), tiles[j])
        for t in rest:
            tiles[t] = jnp.where(inside, 0.0, tiles[t])
        diagonal = jnp.ones_like(panel)
        for k in range(SUBLANES):
            pivot = down(own[k], k)
            diagonal = jnp.where(sub == k, pivot, diagonal)
            reciprocal = 1.0 / pivot
            heads = {i: down(own[i], k) for i in range(k + 1, SUBLANES)}
            row = down(panel, k)
            factor = jnp.where(sub > k, own[k] * reciprocal, 0.0)
            for i in heads:
                own[i] = own[i] - factor * heads[i]
            panel = panel - factor * row
            for t in rest:
                factor = below[t][k] * reciprocal
                for i in heads:
                    below[t][i] = below[t][i] - factor * heads[i]
                tiles[t] = tiles[t] - factor * row
        root = lax.rsqrt(diagonal)
        done = panel * root
        block = jnp.zeros_like(panel)
        for k in range(SUBLANES):
            block = jnp.where(lane == base + k, own[k] * root, block)
        block = jnp.where(lane - base >= sub, block, 0.0)
        here = slice(base, base + SUBLANES)
        upper_ref[here, :] = jnp.where(lane >= base + SUBLANES, done, block)
        inverse_ref[here, :] = jnp.where(lane < base + SUBLANES, done, 0.0)
    basis_ref[...] = dot(sketch_ref[...], inverse_ref[...], ((1,), (1,)), HIGHEST)
    a, b, c, d, e = [sum(piece(40 * t + 8 * i) for t in range(1, count)) + piece(8 * i) for i in range(5)]
    odd = [turned(jnp.where(half, d, c)), turned(jnp.where(half, e, d))]
    mine = jnp.concatenate([a + odd[0], b + odd[1]], axis=0)
    projected_ref[0] = dot(mine, inverse_ref[...], ((1,), (1,)), HIGHEST) * (1.0 / total**0.5)


def factor(parts, sketch, total):
    rows, rank = sketch.shape
    return pl.pallas_call(
        functools.partial(factor_kernel, total),
        in_specs=[WHOLE, WHOLE],
        out_specs=(WHOLE,) * 3,
        out_shape=(
            jax.ShapeDtypeStruct(sketch.shape, F32),
            jax.ShapeDtypeStruct((rank, rank), F32),
            jax.ShapeDtypeStruct((1, 16, rank), F32),
        ),
        scratch_shapes=[pltpu.VMEM((rank, rank), F32)],
        compiler_params=pltpu.CompilerParams(vmem_limit_bytes=LIMIT),
        cost_estimate=cost(50 * 2 * rows * rank * rank, rows * rank, rows * rank),
        name="factor",
    )(parts, sketch)


def exchange(parts, axis):
    return lax.all_to_all(parts, axis, 0, 0)


def body(samples, start_basis):
    rows, columns = samples.shape
    rank = start_basis.shape[1]
    chips, cores, n_col = lax.axis_size("chip"), lax.axis_size("core"), lax.axis_size("col")
    total = rows * chips * cores
    share, gram_share = columns // (chips * cores), rank // chips

    local, samples = sketch_product(samples, start_basis)
    chunks = sum_and_copy(exchange(local.reshape(n_col, rows // n_col, rank), "col"))
    sketch = exchange(chunks, "col").reshape(rows, rank)

    gram, late = lax.optimization_barrier((gram_product(sketch, gram_share), sketch))
    gram = exchange(gram.reshape(chips * cores, gram_share, rank), ("chip", "core")).reshape(2 * rank, rank)
    own, other = wide_product(samples, late, share)
    received = lax.ppermute(other, "core", [(0, 1), (1, 0)])
    packed = pack(gram, own, received).reshape(chips, -1, gram_share, rank)
    parts = exchange(packed, "chip").reshape(-1, rank)
    return factor(parts, sketch, float(total))


def solution(mesh):
    devices = mesh.devices
    split = jax.sharding.Mesh(
        devices.reshape(devices.shape[0] // 2, 2, devices.shape[1]), ("chip", "core", "col")
    )
    row = ("chip", "core")
    in_specs = (P(row, "col"), P("col", None))
    out_specs = (P(row, None), P(), P("col", row, None))
    return jax.shard_map(body, mesh=split, in_specs=in_specs, out_specs=out_specs, check_vma=False)
```

time: 117 us -> 95.5 us (0.82)
  waiting for transfers between devices: 16.8 us -> 0.01 us
  Pallas kernels: 24.1 us -> 10.1 us
  blocking collectives: 64.5 us -> 75.3 us
  starting transfers between devices: 9.38 us -> 5.88 us
  local copies, waits for them, and re-layouts: 0.8 us -> 2.92 us
    all_to_all x2 -> x0, waiting for transfers between devices: 16.8 us -> none  [exchange(): return lax.all_to_all(parts, axis, 0, 0)]
    pallas_call x6 -> x5, Pallas kernels: 22.3 us -> 10.1 us  [the longest x1 5.42 us: factor(): pl.pallas_call(functools.partial(factor_kernel, total), in_specs=[WHOLE,...]
    all_to_all x3 -> x4, blocking collectives: 64.5 us -> 75.3 us  [exchange(): return lax.all_to_all(parts, axis, 0, 0)]
    all_to_all x2 -> x0, starting transfers between devices: 9.38 us -> none  [exchange(): return lax.all_to_all(parts, axis, 0, 0)]
    ppermute x0 -> x1, starting transfers between devices: none -> 5.88 us  [body(): received = lax.ppermute(other, 'core', [(0, 1), (1, 0)])]
    unnamed x4, local copies, waits for them, and re-layouts: 0.8 us -> 2.92 us
    pallas_call x1, Pallas kernels: 1.77 us -> 0.03 us  [sum_and_copy(): pl.pallas_call(sum_kernel, in_specs=[WHOLE], out_specs=WHOLE, out_shape=j...]
  transfers between devices with their start and end apart: 2 -> 1, of which waited for: 2 -> 0; matrix products, arithmetic and copies ran while one was open for 0% -> 0% of each run, Pallas kernels for 9% -> 0%
where the time goes in v3:
time: 95.5 us; the launch traced here: 94.9 us
  blocking collectives  75.3 us (79%)
  Pallas kernels  10.1 us (11%)
  starting transfers between devices  5.88 us (6%)
  local copies, waits for them, and re-layouts  2.92 us (3%)
    all_to_all x4, blocking collectives, exchange(): return lax.all_to_all(parts, axis, 0, 0)  75.3 us
    ppermute x1, starting transfers between devices, body(): received = lax.ppermute(other, 'core', [(0, 1), (1, 0)])  5.88 us
    pallas_call x1, Pallas kernels, factor(): pl.pallas_call(functools.partial(factor_kernel, total), in_specs=[WHOLE,...  5.42 us
    pallas_call x1, Pallas kernels, sketch_product(): pl.pallas_call(functools.partial(sketch_kernel, step), in_specs=[pl.Block...  2.94 us
    unnamed x4, local copies, waits for them, and re-layouts  2.92 us
  transfers between devices with their start and end apart: 1, of which 0 were waited for; matrix products, arithmetic and copies ran while one was open for 0% of the time, Pallas kernels for 0%

profile of v3, /device:TPU:1, one launch (start us, length us, event | category | flops | bytes accessed | tf_op | source)
XLA Modules:
  0.0 94.9 jit_solution(14573936781918142541)
XLA Ops:
  0.6 0.0 copy-start
  0.6 1.9 %copy-done = f32[768,1024]{1,0:T(8,128)S(1)} copy-done((f32[768,1024]{1,0:T(8,128)S(1)}, f32[768,1024]{1,0:T(8,128)}, u32[]{:S(2)}) %copy-start) | copy-done | bytes 3145752
  2.5 0.0 copy-start.1
  2.5 1.0 %copy-done.1 = f32[1024,128]{1,0:T(8,128)S(1)} copy-done((f32[1024,128]{1,0:T(8,128)S(1)}, f32[1024,128]{1,0:T(8,128)}, u32[]{:S(2)}) %copy-start.1) | copy-done | bytes 524312
  3.6 2.9 %sketch_product.1 = (f32[768,128]{1,0:T(8,128)S(1)}, f32[768,1024]{1,0:T(8,128)S(1)}) custom-call(f32[768,1024]{1,0:T(8,128)S(1)} %copy-done, f32[1024,128]{1,0:T(8,128)S(1)} %copy-done.1), custom_call_target="tpu_custom_call" | custom-call | flops 805306368 | bytes 3538944 | tf_op jit(solution)/shard_map/sketch_product/pallas_call | solution.py:62
  6.5 24.2 %all_to_all.20.parts_ref = f32[8,96,128]{2,1,0:T(8,128)S(1)} all-to-all(f32[8,96,128]{2,1,0:T(8,128)S(1)} %bitcast.12), channel_id=1, replica_groups=mesh['chip'=32,'core'=2,'col'=8] {'col'}, dimensions={0} | all-to-all | bytes 786432 | tf_op jit(solution)/shard_map/all_to_all | solution.py:257
  30.7 14.1 %all_to_all.21 = f32[8,96,128]{2,1,0:T(8,128)S(1)} all-to-all(f32[8,96,128]{2,1,0:T(8,128)S(1)} %sum_and_copy.1), channel_id=1, replica_groups=mesh['chip'=32,'core'=2,'col'=8] {'col'}, dimensions={0} | all-to-all | bytes 786432 | tf_op jit(solution)/shard_map/all_to_all | solution.py:257
  44.8 0.5 gram_product.1
  45.4 1.1 %wide_product.1 = (f32[512,128]{1,0:T(8,128)S(1)}, f32[512,128]{1,0:T(8,128)S(1)}) custom-call(f32[768,1024]{1,0:T(8,128)S(1)} %get-tuple-element.11.samples_ref, f32[768,128]{1,0:T(8,128)S(1)} %bitcast.7), custom_call_target="tpu_custom_call" | custom-call | flops 805306368 | bytes 3670016 | tf_op jit(solution)/shard_map/wide_product/pallas_call | solution.py:142
  46.5 5.9 %collective-permute-start = (f32[512,128]{1,0:T(8,128)S(1)}, f32[512,128]{1,0:T(8,128)S(1)}, u32[]{:S(2)}, u32[]{:S(2)}) collective-permute-start(f32[512,128]{1,0:T(8,128)S(1)} %get-tuple-element.14), channel_id=1, source_target_pairs={{0,8},{8,0},{1,9},{9,1},{2,10},{10,2},{3,11},{11,3},{4,12},{12,4},... | collective-permute-start | bytes 786440 | tf_op jit(solution)/shard_map/ppermute | solution.py:274
  52.4 21.1 %all_to_all.22 = f32[64,4,128]{2,1,0:T(4,128)S(1)} all-to-all(f32[64,4,128]{2,1,0:T(4,128)S(1)} %bitcast.11), channel_id=1, replica_groups=mesh['chip'=32,'core'=2,'col'=8] {'chip','core'}, dimensions={0} | all-to-all | bytes 262144 | tf_op jit(solution)/shard_map/all_to_all | solution.py:257
  73.6 0.0 collective-permute-done.received_ref
  73.6 15.8 %all_to_all.23 = f32[32,5,4,128]{3,2,1,0:T(4,128)S(1)} all-to-all(f32[32,5,4,128]{3,2,1,0:T(4,128)S(1)} %bitcast.9), channel_id=1, replica_groups=mesh['chip'=32,'core'=2,'col'=8] {'chip'}, dimensions={0} | all-to-all | bytes 655360 | tf_op jit(solution)/shard_map/all_to_all | solution.py:257
  89.4 5.4 %factor.1 = (f32[768,128]{1,0:T(8,128)}, f32[128,128]{1,0:T(8,128)}, f32[1,16,128]{2,1,0:T(8,128)}) custom-call(f32[640,128]{1,0:T(8,128)S(1)} %bitcast.13, f32[768,128]{1,0:T(8,128)S(1)} %bitcast.8), custom_call_target="tpu_custom_call" | custom-call | flops 1258291200 | bytes 786432 | tf_op jit(solution)/shard_map/factor/pallas_call | solution.py:240
  (2 shorter events, 0.1 us)
Async XLA Ops:
  0.6 1.9 %copy-start = (f32[768,1024]{1,0:T(8,128)S(1)}, f32[768,1024]{1,0:T(8,128)}, u32[]{:S(2)}) copy-start(f32[768,1024]{1,0:T(8,128)} %samples_ref.1) | copy-start | bytes 9437188
  2.5 1.0 %copy-start.1 = (f32[1024,128]{1,0:T(8,128)S(1)}, f32[1024,128]{1,0:T(8,128)}, u32[]{:S(2)}) copy-start(f32[1024,128]{1,0:T(8,128)} %start_ref.1) | copy-start | bytes 1572868
  46.5 27.0 %collective-permute-start = (f32[512,128]{1,0:T(8,128)S(1)}, f32[512,128]{1,0:T(8,128)S(1)}, u32[]{:S(2)}, u32[]{:S(2)}) collective-permute-start(f32[512,128]{1,0:T(8,128)S(1)} %get-tuple-element.14), channel_id=1, source_target_pairs={{0,8},{8,0},{1,9},{9,1},{2,10},{10,2},{3,11},{11,3},{4,12},{12,4},... | collective-permute-start | bytes 786440 | tf_op jit(solution)/shard_map/ppermute | solution.py:274

commit v4 on v3

v4 whole, which is shorter than its diff:
```python
import functools

import jax
import jax.numpy as jnp
from jax import lax
from jax.experimental import pallas as pl
from jax.experimental.pallas import tpu as pltpu
from jax.sharding import PartitionSpec as P

F32, BF16 = jnp.float32, jnp.bfloat16
HIGHEST = lax.Precision.HIGHEST
WHOLE = pl.BlockSpec(memory_space=pltpu.VMEM)
SUBLANES = 8
LIMIT = 12 * 2**20


def halves(values):
    high = values.astype(BF16)
    return high, (values - high.astype(F32)).astype(BF16)


def dot(left, right, axes, precision=None):
    return lax.dot_general(
        left, right, (axes, ((), ())), precision=precision, preferred_element_type=F32
    )


def cost(flops, read, written):
    return pl.CostEstimate(flops=flops, bytes_accessed=4 * (read + written), transcendentals=0)


def split_dot(left, right_halves, axes):
    high, low = halves(left)
    both = dot(high, right_halves, axes) + dot(low, right_halves, axes)
    rank = right_halves.shape[1] // 2
    return both[:, :rank] + both[:, rank:]


def sketch_kernel(step, block, samples_ref, start_ref, local_ref, held_ref, start, sems):
    rows, columns = held_ref.shape
    rank = local_ref.shape[1]
    copies = []
    for i in range(columns // step):
        at = pl.ds(i * step, step)
        pair = (
            pltpu.make_async_copy(start_ref.at[at], start.at[at], sems.at[0, i]),
            pltpu.make_async_copy(samples_ref.at[:, at], held_ref.at[:, at], sems.at[1, i]),
        )
        for copy in pair:
            copy.start()
        copies.append(pair)
    for i, pair in enumerate(copies):
        for copy in pair:
            copy.wait()
        at = slice(i * step, (i + 1) * step)
        right = jnp.concatenate(halves(start[at]), axis=1)
        for first in range(0, rows, block):
            here = slice(first, first + block)
            left = jnp.concatenate(halves(held_ref[here, at]), axis=0)
            both = dot(left, right, ((1,), (0,)))
            both = both[:block] + both[block:]
            both = both[:, :rank] + both[:, rank:]
            local_ref[here] = both if i == 0 else local_ref[here] + both


def sketch_product(samples, start_basis, step=256, block=128):
    rows, columns = samples.shape
    rank = start_basis.shape[1]
    samples, start_basis = (
        pltpu.with_memory_space_constraint(values, pltpu.HBM) for values in (samples, start_basis)
    )
    return pl.pallas_call(
        functools.partial(sketch_kernel, step, block),
        in_specs=[pl.BlockSpec(memory_space=pltpu.HBM)] * 2,
        out_specs=(WHOLE, WHOLE),
        out_shape=(
            jax.ShapeDtypeStruct((rows, rank), F32),
            jax.ShapeDtypeStruct((rows, columns), F32),
        ),
        scratch_shapes=[
            pltpu.VMEM((columns, rank), F32),
            pltpu.SemaphoreType.DMA((2, columns // step)),
        ],
        compiler_params=pltpu.CompilerParams(vmem_limit_bytes=LIMIT),
        cost_estimate=cost(8 * rows * columns * rank, rows * columns, rows * rank),
        name="sketch_product",
    )(samples, start_basis)


def sum_kernel(parts_ref, out_ref):
    total = parts_ref[0]
    for i in range(1, parts_ref.shape[0]):
        total = total + parts_ref[i]
    for i in range(out_ref.shape[0]):
        out_ref[i] = total


def sum_and_copy(parts):
    return pl.pallas_call(
        sum_kernel,
        in_specs=[WHOLE],
        out_specs=WHOLE,
        out_shape=jax.ShapeDtypeStruct(parts.shape, F32),
        compiler_params=pltpu.CompilerParams(vmem_limit_bytes=LIMIT),
        cost_estimate=cost(parts.size, parts.size, parts.size),
        name="sum_and_copy",
    )(parts)


def products_kernel(step, share, samples_ref, sketch_ref, own_ref, other_ref, sketch_halves):
    core = lax.axis_index("core")
    rank = sketch_ref.shape[1]

    def give(at, for_first, for_second):
        here = slice(at, at + for_first.shape[0])
        own_ref[here] = jnp.where(core == 0, for_first, for_second)
        other_ref[here] = jnp.where(core == 0, for_second, for_first)

    sketch = sketch_ref[...]
    gram = dot(sketch, sketch, ((0,), (0,)), HIGHEST)
    tiles = [gram[at : at + SUBLANES] for at in range(0, rank, SUBLANES)]
    packed = packed_tiles(tiles)
    middle = len(packed) // 2 + 1
    first, second = packed[:middle], packed[middle:]
    second += [jnp.zeros_like(gram[:SUBLANES])] * (len(first) - len(second))
    for i, pair in enumerate(zip(first, second)):
        give(samples_ref.shape[1] // 2 + SUBLANES * i, *pair)

    high, low = halves(sketch)
    sketch_halves[:, :rank] = high
    sketch_halves[:, rank:] = low
    for at in range(0, samples_ref.shape[1], step):
        wide = split_dot(samples_ref[:, at : at + step], sketch_halves[...], ((0,), (0,)))
        for begin in range(0, step, 2 * share):
            pair = [wide[begin + share * i : begin + share * (i + 1)] for i in range(2)]
            give((at + begin) // 2, *pair)


def packed_tiles(tiles):
    count, size = len(tiles), tiles[0].shape[1]
    lane = lax.broadcasted_iota(jnp.int32, tiles[0].shape, 1)
    packed = [tiles[0]]
    for t in range(1, count // 2):
        start = SUBLANES * t
        packed.append(jnp.where(lane >= start, tiles[t], pltpu.roll(tiles[count - t], start, 1)))
    return packed + [tiles[count // 2]]


def unpacked_tiles(packed):
    count, size = 2 * (len(packed) - 1), packed[0].shape[1]
    tiles = list(packed) + [None] * (count - len(packed))
    for t in range(1, count // 2):
        tiles[count - t] = pltpu.roll(packed[t], size - SUBLANES * t, 1)
    upper = jnp.concatenate(tiles, axis=0)
    row = lax.broadcasted_iota(jnp.int32, upper.shape, 0)
    lane = lax.broadcasted_iota(jnp.int32, upper.shape, 1)
    whole = jnp.where(lane >= row // SUBLANES * SUBLANES, upper, upper.T)
    return [whole[at : at + SUBLANES] for at in range(0, size, SUBLANES)]


def gram_rows(rank):
    return SUBLANES * (rank // SUBLANES // 4 + 1)


def products(samples, sketch, share, step=256):
    rows, columns = samples.shape
    rank = sketch.shape[1]
    half = jax.ShapeDtypeStruct((columns // 2 + gram_rows(rank), rank), F32)
    return pl.pallas_call(
        functools.partial(products_kernel, step, share),
        in_specs=[WHOLE, WHOLE],
        out_specs=(WHOLE, WHOLE),
        out_shape=(half, half),
        scratch_shapes=[pltpu.VMEM((rows, 2 * rank), BF16)],
        compiler_params=pltpu.CompilerParams(vmem_limit_bytes=LIMIT),
        cost_estimate=cost(8 * rows * columns * rank, rows * columns, columns * rank),
        name="products",
    )(samples, sketch)


def added(refs, at, rows):
    total = refs[0][at : at + rows]
    for ref in refs[1:]:
        total = total + ref[at : at + rows]
    return total


def spread_kernel(share, inner, outer, gram, *refs):
    *parts, out_ref = refs
    last = added(parts, outer * inner * share, gram)
    size = outer * share + gram
    for i in range(inner):
        for o in range(outer):
            here = size * i + share * o
            out_ref[here : here + share] = added(parts, (o * inner + i) * share, share)
        out_ref[size * (i + 1) - gram : size * (i + 1)] = last


def spread(parts, share, inner, gram):
    rows, rank = parts[0].shape
    outer = (rows - gram) // share // inner
    size = outer * share + gram
    out = pl.pallas_call(
        functools.partial(spread_kernel, share, inner, outer, gram),
        in_specs=[WHOLE] * len(parts),
        out_specs=WHOLE,
        out_shape=jax.ShapeDtypeStruct((inner * size, rank), F32),
        compiler_params=pltpu.CompilerParams(vmem_limit_bytes=LIMIT),
        cost_estimate=cost(rows * rank, rows * rank, inner * size * rank),
        name="spread",
    )(*parts)
    return out.reshape(inner, size, rank)


def respread_kernel(share, count, gram, parts_ref, out_ref):
    parts = [parts_ref.at[i] for i in range(parts_ref.shape[0])]
    last = added(parts, count * share, gram)
    for i in range(count):
        out_ref[i, :share] = added(parts, i * share, share)
        out_ref[i, share:] = last


def respread(parts, share, gram):
    count = (parts.shape[1] - gram) // share
    rank = parts.shape[2]
    return pl.pallas_call(
        functools.partial(respread_kernel, share, count, gram),
        in_specs=[WHOLE],
        out_specs=WHOLE,
        out_shape=jax.ShapeDtypeStruct((count, share + gram, rank), F32),
        compiler_params=pltpu.CompilerParams(vmem_limit_bytes=LIMIT),
        cost_estimate=cost(parts.size, parts.size, parts.size),
        name="respread",
    )(parts)


def finish_kernel(parts_ref, mine_ref, gram_ref):
    parts = [parts_ref.at[i] for i in range(parts_ref.shape[0])]
    share, gram = mine_ref.shape[0], gram_ref.shape[0]
    mine_ref[...] = added(parts, 0, share)
    gram_ref[...] = added(parts, share, gram)


def finish(parts, share):
    rows, rank = parts.shape[1:]
    return pl.pallas_call(
        finish_kernel,
        in_specs=[WHOLE],
        out_specs=(WHOLE, WHOLE),
        out_shape=(
            jax.ShapeDtypeStruct((share, rank), F32),
            jax.ShapeDtypeStruct((rows - share, rank), F32),
        ),
        compiler_params=pltpu.CompilerParams(vmem_limit_bytes=LIMIT),
        cost_estimate=cost(parts.size, parts.size, rows * rank),
        name="finish",
    )(parts)


def factor_kernel(
    total, packed_ref, mine_ref, sketch_ref, basis_ref, upper_ref, projected_ref, inverse_ref
):
    size = upper_ref.shape[0]
    count = size // SUBLANES
    lane = lax.broadcasted_iota(jnp.int32, (SUBLANES, size), 1)
    sub = lax.broadcasted_iota(jnp.int32, (SUBLANES, size), 0)
    down = lambda values, row: jnp.broadcast_to(values[row : row + 1, :], values.shape)
    across = lambda values, column: jnp.broadcast_to(values[:, column : column + 1], values.shape)
    packed = [packed_ref[SUBLANES * i : SUBLANES * (i + 1)] for i in range(count // 2 + 1)]
    tiles = [tile / total for tile in unpacked_tiles(packed)]
    for j in range(count):
        base = SUBLANES * j
        inside = (lane >= base) & (lane < base + SUBLANES)
        rest = range(j + 1, count)
        own = [across(tiles[j], base + k) for k in range(SUBLANES)]
        below = {t: [across(tiles[t], base + k) for k in range(SUBLANES)] for t in rest}
        panel = jnp.where(inside, jnp.where(lane - base == sub, 1.0, 0.0), tiles[j])
        for t in rest:
            tiles[t] = jnp.where(inside, 0.0, tiles[t])
        diagonal = jnp.ones_like(panel)
        for k in range(SUBLANES):
            pivot = down(own[k], k)
            diagonal = jnp.where(sub == k, pivot, diagonal)
            reciprocal = 1.0 / pivot
            heads = {i: down(own[i], k) for i in range(k + 1, SUBLANES)}
            row = down(panel, k)
            factor = jnp.where(sub > k, own[k] * reciprocal, 0.0)
            for i in heads:
                own[i] = own[i] - factor * heads[i]
            panel = panel - factor * row
            for t in rest:
                factor = below[t][k] * reciprocal
                for i in heads:
                    below[t][i] = below[t][i] - factor * heads[i]
                tiles[t] = tiles[t] - factor * row
        root = lax.rsqrt(diagonal)
        done = panel * root
        block = jnp.zeros_like(panel)
        for k in range(SUBLANES):
            block = jnp.where(lane == base + k, own[k] * root, block)
        block = jnp.where(lane - base >= sub, block, 0.0)
        here = slice(base, base + SUBLANES)
        upper_ref[here, :] = jnp.where(lane >= base + SUBLANES, done, block)
        inverse_ref[here, :] = jnp.where(lane < base + SUBLANES, done, 0.0)
    basis_ref[...] = dot(sketch_ref[...], inverse_ref[...], ((1,), (1,)), HIGHEST)
    projected_ref[0] = dot(mine_ref[...], inverse_ref[...], ((1,), (1,)), HIGHEST) * (1.0 / total**0.5)


def factor(packed, mine, sketch, total):
    rows, rank = sketch.shape
    return pl.pallas_call(
        functools.partial(factor_kernel, total),
        in_specs=[WHOLE] * 3,
        out_specs=(WHOLE,) * 3,
        out_shape=(
            jax.ShapeDtypeStruct(sketch.shape, F32),
            jax.ShapeDtypeStruct((rank, rank), F32),
            jax.ShapeDtypeStruct((1,) + mine.shape, F32),
        ),
        scratch_shapes=[pltpu.VMEM((rank, rank), F32)],
        compiler_params=pltpu.CompilerParams(vmem_limit_bytes=LIMIT),
        cost_estimate=cost(50 * 2 * rows * rank * rank, rows * rank, rows * rank),
        name="factor",
    )(packed, mine, sketch)


def exchange(parts, axis):
    return lax.all_to_all(parts, axis, 0, 0)


def body(samples, start_basis):
    rows, columns = samples.shape
    rank = start_basis.shape[1]
    y, x, cores, n_col = (lax.axis_size(name) for name in ("y", "x", "core", "col"))
    total = rows * y * x * cores
    share, gram = columns // (y * x * cores), gram_rows(rank)

    local, samples = sketch_product(samples, start_basis)
    chunks = sum_and_copy(exchange(local.reshape(n_col, rows // n_col, rank), "col"))
    sketch = exchange(chunks, "col").reshape(rows, rank)

    own, other = products(samples, sketch, share)
    received = lax.ppermute(other, "core", [(0, 1), (1, 0)])
    parts = exchange(spread([own, received], share, x, gram), "x")
    parts = exchange(respread(parts, share, gram), "y")
    mine, half = finish(parts, share)
    packed = lax.all_gather(half, "core", axis=0, tiled=True)
    return factor(packed, mine, sketch, float(total))


def solution(mesh):
    split = jax.sharding.Mesh(mesh.devices.reshape(8, 4, 2, 8), ("y", "x", "core", "col"))
    row = ("y", "x", "core")
    in_specs = (P(row, "col"), P("col", None))
    out_specs = (P(row, None), P(), P("col", row, None))
    return jax.shard_map(body, mesh=split, in_specs=in_specs, out_specs=out_specs, check_vma=False)
```

time: 95.5 us -> 87.3 us (0.914)
  blocking collectives: 75.3 us -> 69.3 us
  local copies, waits for them, and re-layouts: 2.92 us -> 0 us
  waiting for transfers between devices: 0.01 us -> 1.17 us
    all_to_all x4, blocking collectives: 75.3 us -> 64.6 us  [exchange(): return lax.all_to_all(parts, axis, 0, 0)]
    all_gather x0 -> x1, blocking collectives: none -> 4.77 us  [body(): packed = lax.all_gather(half, 'core', axis=0, tiled=True)]
    unnamed x4 -> x0, local copies, waits for them, and re-layouts: 2.92 us -> none
    ppermute x1, waiting for transfers between devices: 0.01 us -> 1.17 us  [body(): received = lax.ppermute(other, 'core', [(0, 1), (1, 0)])]
    pallas_call x5 -> x6, Pallas kernels: 10.1 us -> 9.97 us  [the longest x1 5.53 us: factor(): pl.pallas_call(functools.partial(factor_kernel, total), in_specs=[WHOLE]...]
  transfers between devices with their start and end apart: 1 -> 1, of which waited for: 0 -> 1; matrix products, arithmetic and copies ran while one was open for 0% -> 0% of each run, Pallas kernels for 0% -> 0%
where the time goes in v4:
time: 87.3 us; the launch traced here: 87.1 us
  blocking collectives  69.3 us (79%)
  Pallas kernels  10 us (11%)
  starting transfers between devices  5.88 us (7%)
  waiting for transfers between devices  1.17 us (1%)
    all_to_all x4, blocking collectives, exchange(): return lax.all_to_all(parts, axis, 0, 0)  64.6 us
    ppermute x1, starting transfers between devices, body(): received = lax.ppermute(other, 'core', [(0, 1), (1, 0)])  5.88 us
    pallas_call x1, Pallas kernels, factor(): pl.pallas_call(functools.partial(factor_kernel, total), in_specs=[WHOLE]...  5.53 us
    all_gather x1, blocking collectives, body(): packed = lax.all_gather(half, 'core', axis=0, tiled=True)  4.77 us
    pallas_call x1, Pallas kernels, sketch_product(): pl.pallas_call(functools.partial(sketch_kernel, step, block), in_specs=[p...  2.82 us
  transfers between devices with their start and end apart: 1, of which 1 were waited for; matrix products, arithmetic and copies ran while one was open for 0% of the time, Pallas kernels for 0%

profile of v4, /device:TPU:1, one launch (start us, length us, event | category | flops | bytes accessed | tf_op | source)
XLA Modules:
  0.0 87.1 jit_solution(18417343697555774056)
XLA Ops:
  0.6 2.8 %sketch_product.1 = (f32[768,128]{1,0:T(8,128)S(1)}, f32[768,1024]{1,0:T(8,128)S(1)}) custom-call(f32[768,1024]{1,0:T(8,128)} %samples_ref.1, f32[1024,128]{1,0:T(8,128)} %start_ref.1), custom_call_target="tpu_custom_call" | custom-call | flops 805306368 | bytes 3538944 | tf_op jit(solution)/shard_map/sketch_product/pallas_call | solution.py:72
  3.5 24.2 %all_to_all.20.parts_ref = f32[8,96,128]{2,1,0:T(8,128)S(1)} all-to-all(f32[8,96,128]{2,1,0:T(8,128)S(1)} %bitcast.6), channel_id=1, replica_groups=mesh['y'=8,'x'=4,'core'=2,'col'=8] {'col'}, dimensions={0} | all-to-all | bytes 786432 | tf_op jit(solution)/shard_map/all_to_all | solution.py:328
  27.7 14.1 %all_to_all.21 = f32[8,96,128]{2,1,0:T(8,128)S(1)} all-to-all(f32[8,96,128]{2,1,0:T(8,128)S(1)} %sum_and_copy.1), channel_id=1, replica_groups=mesh['y'=8,'x'=4,'core'=2,'col'=8] {'col'}, dimensions={0} | all-to-all | bytes 786432 | tf_op jit(solution)/shard_map/all_to_all | solution.py:328
  41.8 1.5 %products.1 = (f32[552,128]{1,0:T(8,128)S(1)}, f32[552,128]{1,0:T(8,128)S(1)}) custom-call(f32[768,1024]{1,0:T(8,128)S(1)} %get-tuple-element.9.samples_ref, f32[768,128]{1,0:T(8,128)S(1)} %bitcast.3), custom_call_target="tpu_custom_call" | custom-call | flops 805306368 | bytes 3670016 | tf_op jit(solution)/shard_map/products/pallas_call | solution.py:169
  43.3 5.9 %collective-permute-start = (f32[552,128]{1,0:T(8,128)S(1)}, f32[552,128]{1,0:T(8,128)S(1)}, u32[]{:S(2)}, u32[]{:S(2)}) collective-permute-start(f32[552,128]{1,0:T(8,128)S(1)} %get-tuple-element.12), channel_id=1, source_target_pairs={{0,8},{8,0},{1,9},{9,1},{2,10},{10,2},{3,11},{11,3},{4,12},{12,4},... | collective-permute-start | bytes 847880 | tf_op jit(solution)/shard_map/ppermute | solution.py:343
  49.2 1.2 %collective-permute-done.refs_1_ = f32[552,128]{1,0:T(8,128)S(1)} collective-permute-done((f32[552,128]{1,0:T(8,128)S(1)}, f32[552,128]{1,0:T(8,128)S(1)}, u32[]{:S(2)}, u32[]{:S(2)}) %collective-permute-start) | collective-permute-done | bytes 282656 | tf_op jit(solution)/shard_map/ppermute | solution.py:343
  50.4 10.8 %all_to_all.22.parts_ref = f32[4,168,128]{2,1,0:T(8,128)S(1)} all-to-all(f32[4,168,128]{2,1,0:T(8,128)S(1)} %bitcast.5), channel_id=1, replica_groups=mesh['y'=8,'x'=4,'core'=2,'col'=8] {'x'}, dimensions={0} | all-to-all | bytes 688128 | tf_op jit(solution)/shard_map/all_to_all | solution.py:328
  61.2 15.5 %all_to_all.23.parts_ref = f32[8,56,128]{2,1,0:T(8,128)S(1)} all-to-all(f32[8,56,128]{2,1,0:T(8,128)S(1)} %respread.1), channel_id=1, replica_groups=mesh['y'=8,'x'=4,'core'=2,'col'=8] {'y'}, dimensions={0} | all-to-all | bytes 458752 | tf_op jit(solution)/shard_map/all_to_all | solution.py:328
  76.8 4.8 %all_gather.3.packed_ref = f32[80,128]{1,0:T(8,128)S(1)} all-gather(f32[40,128]{1,0:T(8,128)S(1)} %get-tuple-element.13), channel_id=1, replica_groups=mesh['y'=8,'x'=4,'core'=2,'col'=8] {'core'}, dimensions={0}, use_global_device_ids=true | all-gather | bytes 61440 | tf_op jit(solution)/shard_map/all_gather | solution.py:347
  81.5 5.5 %factor.1 = (f32[768,128]{1,0:T(8,128)}, f32[128,128]{1,0:T(8,128)}, f32[1,16,128]{2,1,0:T(8,128)}) custom-call(f32[80,128]{1,0:T(8,128)S(1)} %all_gather.3.packed_ref, f32[16,128]{1,0:T(8,128)S(1)} %get-tuple-element.14.mine_ref, f32[768,128]{1,0:T(8,128)S(1)} %bitcast.4), custom_call_target="tpu_custom_call" | custom-call | flops 1258291200 | bytes 786432 | tf_op jit(solution)/shard_map/factor/pallas_call | solution.py:311
  (4 shorter events, 0.1 us)
Async XLA Ops:
  43.3 7.1 %collective-permute-start = (f32[552,128]{1,0:T(8,128)S(1)}, f32[552,128]{1,0:T(8,128)S(1)}, u32[]{:S(2)}, u32[]{:S(2)}) collective-permute-start(f32[552,128]{1,0:T(8,128)S(1)} %get-tuple-element.12), channel_id=1, source_target_pairs={{0,8},{8,0},{1,9},{9,1},{2,10},{10,2},{3,11},{11,3},{4,12},{12,4},... | collective-permute-start | bytes 847880 | tf_op jit(solution)/shard_map/ppermute | solution.py:343

commit v5 on v4

--- a/solution.py
+++ b/solution.py
@@ -185,30 +185,36 @@
     return total
 
 
-def spread_kernel(share, inner, outer, gram, *refs):
-    *parts, out_ref = refs
-    last = added(parts, outer * inner * share, gram)
+def spread_kernel(share, inner, outer, gram, own_ref, others_ref, out_ref):
+    rows = own_ref.shape[0]
+    theirs = (1 - lax.axis_index("core")) * rows
+
+    def total(at, count):
+        there = pl.ds(pl.multiple_of(theirs + at, SUBLANES), count)
+        return own_ref[at : at + count] + others_ref[there]
+
+    last = total(outer * inner * share, gram)
     size = outer * share + gram
     for i in range(inner):
         for o in range(outer):
             here = size * i + share * o
-            out_ref[here : here + share] = added(parts, (o * inner + i) * share, share)
+            out_ref[here : here + share] = total((o * inner + i) * share, share)
         out_ref[size * (i + 1) - gram : size * (i + 1)] = last
 
 
-def spread(parts, share, inner, gram):
-    rows, rank = parts[0].shape
+def spread(own, others, share, inner, gram):
+    rows, rank = own.shape
     outer = (rows - gram) // share // inner
     size = outer * share + gram
     out = pl.pallas_call(
         functools.partial(spread_kernel, share, inner, outer, gram),
-        in_specs=[WHOLE] * len(parts),
+        in_specs=[WHOLE] * 2,
         out_specs=WHOLE,
         out_shape=jax.ShapeDtypeStruct((inner * size, rank), F32),
         compiler_params=pltpu.CompilerParams(vmem_limit_bytes=LIMIT),
         cost_estimate=cost(rows * rank, rows * rank, inner * size * rank),
         name="spread",
-    )(*parts)
+    )(own, others)
     return out.reshape(inner, size, rank)
 
 
@@ -268,38 +274,61 @@
     across = lambda values, column: jnp.broadcast_to(values[:, column : column + 1], values.shape)
     packed = [packed_ref[SUBLANES * i : SUBLANES * (i + 1)] for i in range(count // 2 + 1)]
     tiles = [tile / total for tile in unpacked_tiles(packed)]
+    columns = lambda t, j: [across(tiles[t], SUBLANES * j + k) for k in range(SUBLANES)]
+    own, below = columns(0, 0), {1: columns(1, 0)}
     for j in range(count):
         base = SUBLANES * j
+        here = slice(base, base + SUBLANES)
         inside = (lane >= base) & (lane < base + SUBLANES)
-        rest = range(j + 1, count)
-        own = [across(tiles[j], base + k) for k in range(SUBLANES)]
-        below = {t: [across(tiles[t], base + k) for k in range(SUBLANES)] for t in rest}
+        near = range(j + 1, min(j + 1 + 4, count))
+        for t in near[1:]:
+            below[t] = columns(t, j)
+        ahead = [columns(t, j + 1) for t in near[:2]]
+        terms = [[None] * SUBLANES for t in near[:2]]
         panel = jnp.where(inside, jnp.where(lane - base == sub, 1.0, 0.0), tiles[j])
-        for t in rest:
+        for t in range(j + 1, count):
             tiles[t] = jnp.where(inside, 0.0, tiles[t])
         diagonal = jnp.ones_like(panel)
         for k in range(SUBLANES):
+            later = range(k + 1, SUBLANES)
             pivot = down(own[k], k)
+            reciprocal = 1.0 / pivot
+            heads = {i: down(own[i], k) for i in later}
             diagonal = jnp.where(sub == k, pivot, diagonal)
-            reciprocal = 1.0 / pivot
-            heads = {i: down(own[i], k) for i in range(k + 1, SUBLANES)}
             row = down(panel, k)
             factor = jnp.where(sub > k, own[k] * reciprocal, 0.0)
-            for i in heads:
+            for i in later:
                 own[i] = own[i] - factor * heads[i]
             panel = panel - factor * row
-            for t in rest:
+            for t in near:
                 factor = below[t][k] * reciprocal
-                for i in heads:
+                for i in later:
                     below[t][i] = below[t][i] - factor * heads[i]
                 tiles[t] = tiles[t] - factor * row
+                if t < j + 3:
+                    for i in range(SUBLANES):
+                        term = factor * down(below[j + 1][k], i)
+                        known = terms[t - j - 1][i]
+                        terms[t - j - 1][i] = term if known is None else known + term
+        ahead = [[v - u for v, u in zip(*pair)] for pair in zip(ahead, terms)]
+        owned = own
+        if ahead:
+            own, below = ahead[0], {j + 2: ahead[-1]}
         root = lax.rsqrt(diagonal)
         done = panel * root
+        if near and near[-1] + 1 < count:
+            first = done.astype(BF16).astype(F32)
+            second = (done - first).astype(BF16).astype(F32)
+            third = done - first - second
+            left = jnp.concatenate([first, first, second, first, third, second], axis=0).astype(BF16)
+            right = jnp.concatenate([first, second, first, third, first, second], axis=0).astype(BF16)
+            update = dot(left, right, ((0,), (0,)))
+            for t in range(near[-1] + 1, count):
+                tiles[t] = tiles[t] - update[SUBLANES * t : SUBLANES * (t + 1)]
         block = jnp.zeros_like(panel)
         for k in range(SUBLANES):
-            block = jnp.where(lane == base + k, own[k] * root, block)
+            block = jnp.where(lane == base + k, owned[k] * root, block)
         block = jnp.where(lane - base >= sub, block, 0.0)
-        here = slice(base, base + SUBLANES)
         upper_ref[here, :] = jnp.where(lane >= base + SUBLANES, done, block)
         inverse_ref[here, :] = jnp.where(lane < base + SUBLANES, done, 0.0)
     basis_ref[...] = dot(sketch_ref[...], inverse_ref[...], ((1,), (1,)), HIGHEST)
@@ -340,8 +369,8 @@
     sketch = exchange(chunks, "col").reshape(rows, rank)
 
     own, other = products(samples, sketch, share)
-    received = lax.ppermute(other, "core", [(0, 1), (1, 0)])
-    parts = exchange(spread([own, received], share, x, gram), "x")
+    others = lax.all_gather(other, "core", axis=0, tiled=True)
+    parts = exchange(spread(own, others, share, x, gram), "x")
     parts = exchange(respread(parts, share, gram), "y")
     mine, half = finish(parts, share)
     packed = lax.all_gather(half, "core", axis=0, tiled=True)

time: 87.3 us -> 84.5 us (0.968)
  starting transfers between devices: 5.88 us -> 0 us
  blocking collectives: 69.3 us -> 75.1 us
  Pallas kernels: 10 us -> 8.48 us
  waiting for transfers between devices: 1.17 us -> 0 us
    ppermute x1 -> x0, starting transfers between devices: 5.88 us -> none  [body(): received = lax.ppermute(other, 'core', [(0, 1), (1, 0)])]
    all_gather x0 -> x1, blocking collectives: none -> 5.81 us  [body(): others = lax.all_gather(other, 'core', axis=0, tiled=True)]
    pallas_call x1, Pallas kernels: 5.53 us -> 4 us  [factor(): pl.pallas_call(functools.partial(factor_kernel, total), in_specs=[WHOLE]...]
    ppermute x1 -> x0, waiting for transfers between devices: 1.17 us -> none  [body(): received = lax.ppermute(other, 'core', [(0, 1), (1, 0)])]
  transfers between devices with their start and end apart: 1 -> 0, of which waited for: 1 -> 0; matrix products, arithmetic and copies ran while one was open for 0% -> 0% of each run, Pallas kernels for 0% -> 0%
where the time goes in v5:
time: 84.5 us; the launch traced here: 84.3 us
  blocking collectives  75.1 us (89%)
  Pallas kernels  8.48 us (10%)
    all_to_all x4, blocking collectives, exchange(): return lax.all_to_all(parts, axis, 0, 0)  64.6 us
    all_gather x1, blocking collectives, body(): others = lax.all_gather(other, 'core', axis=0, tiled=True)  5.81 us
    all_gather x1, blocking collectives, body(): packed = lax.all_gather(half, 'core', axis=0, tiled=True)  4.77 us
    pallas_call x1, Pallas kernels, factor(): pl.pallas_call(functools.partial(factor_kernel, total), in_specs=[WHOLE]...  4 us
    pallas_call x1, Pallas kernels, sketch_product(): pl.pallas_call(functools.partial(sketch_kernel, step, block), in_specs=[p...  2.82 us

profile of v5, /device:TPU:1, one launch (start us, length us, event | category | flops | bytes accessed | tf_op | source)
XLA Modules:
  0.0 84.3 jit_solution(8077674288283597562)
XLA Ops:
  0.6 2.8 %sketch_product.1 = (f32[768,128]{1,0:T(8,128)S(1)}, f32[768,1024]{1,0:T(8,128)S(1)}) custom-call(f32[768,1024]{1,0:T(8,128)} %samples_ref.1, f32[1024,128]{1,0:T(8,128)} %start_ref.1), custom_call_target="tpu_custom_call" | custom-call | flops 805306368 | bytes 3538944 | tf_op jit(solution)/shard_map/sketch_product/pallas_call | solution.py:72
  3.5 24.2 %all_to_all.20.parts_ref = f32[8,96,128]{2,1,0:T(8,128)S(1)} all-to-all(f32[8,96,128]{2,1,0:T(8,128)S(1)} %bitcast.6), channel_id=1, replica_groups=mesh['y'=8,'x'=4,'core'=2,'col'=8] {'col'}, dimensions={0} | all-to-all | bytes 786432 | tf_op jit(solution)/shard_map/all_to_all | solution.py:357
  27.7 14.1 %all_to_all.21 = f32[8,96,128]{2,1,0:T(8,128)S(1)} all-to-all(f32[8,96,128]{2,1,0:T(8,128)S(1)} %sum_and_copy.1), channel_id=1, replica_groups=mesh['y'=8,'x'=4,'core'=2,'col'=8] {'col'}, dimensions={0} | all-to-all | bytes 786432 | tf_op jit(solution)/shard_map/all_to_all | solution.py:357
  41.8 1.6 %products.1 = (f32[552,128]{1,0:T(8,128)S(1)}, f32[552,128]{1,0:T(8,128)S(1)}) custom-call(f32[768,1024]{1,0:T(8,128)S(1)} %get-tuple-element.9.samples_ref, f32[768,128]{1,0:T(8,128)S(1)} %bitcast.3), custom_call_target="tpu_custom_call" | custom-call | flops 805306368 | bytes 3670016 | tf_op jit(solution)/shard_map/products/pallas_call | solution.py:169
  43.4 5.8 %all_gather.6.others_ref = f32[1104,128]{1,0:T(8,128)S(1)} all-gather(f32[552,128]{1,0:T(8,128)S(1)} %get-tuple-element.12), channel_id=1, replica_groups=mesh['y'=8,'x'=4,'core'=2,'col'=8] {'core'}, dimensions={0}, use_global_device_ids=true | all-gather | bytes 847872 | tf_op jit(solution)/shard_map/all_gather | solution.py:372
  49.2 10.8 %all_to_all.22.parts_ref = f32[4,168,128]{2,1,0:T(8,128)S(1)} all-to-all(f32[4,168,128]{2,1,0:T(8,128)S(1)} %bitcast.5), channel_id=1, replica_groups=mesh['y'=8,'x'=4,'core'=2,'col'=8] {'x'}, dimensions={0} | all-to-all | bytes 688128 | tf_op jit(solution)/shard_map/all_to_all | solution.py:357
  60.0 15.5 %all_to_all.23.parts_ref = f32[8,56,128]{2,1,0:T(8,128)S(1)} all-to-all(f32[8,56,128]{2,1,0:T(8,128)S(1)} %respread.1), channel_id=1, replica_groups=mesh['y'=8,'x'=4,'core'=2,'col'=8] {'y'}, dimensions={0} | all-to-all | bytes 458752 | tf_op jit(solution)/shard_map/all_to_all | solution.py:357
  75.5 4.8 %all_gather.7.packed_ref = f32[80,128]{1,0:T(8,128)S(1)} all-gather(f32[40,128]{1,0:T(8,128)S(1)} %get-tuple-element.13), channel_id=1, replica_groups=mesh['y'=8,'x'=4,'core'=2,'col'=8] {'core'}, dimensions={0}, use_global_device_ids=true | all-gather | bytes 61440 | tf_op jit(solution)/shard_map/all_gather | solution.py:376
  80.3 4.0 %factor.1 = (f32[768,128]{1,0:T(8,128)}, f32[128,128]{1,0:T(8,128)}, f32[1,16,128]{2,1,0:T(8,128)}) custom-call(f32[80,128]{1,0:T(8,128)S(1)} %all_gather.7.packed_ref, f32[16,128]{1,0:T(8,128)S(1)} %get-tuple-element.14.mine_ref, f32[768,128]{1,0:T(8,128)S(1)} %bitcast.4), custom_call_target="tpu_custom_call" | custom-call | flops 1258291200 | bytes 786432 | tf_op jit(solution)/shard_map/factor/pallas_call | solution.py:340
  (4 shorter events, 0.1 us)

commit v6 on v5

--- a/solution.py
+++ b/solution.py
@@ -19,6 +19,12 @@
     return high, (values - high.astype(F32)).astype(BF16)
 
 
+def thirds(values):
+    high, rest = values.astype(BF16), values - values.astype(BF16).astype(F32)
+    middle = rest.astype(BF16)
+    return [high, middle, (rest - middle.astype(F32)).astype(BF16)]
+
+
 def dot(left, right, axes, precision=None):
     return lax.dot_general(
         left, right, (axes, ((), ())), precision=precision, preferred_element_type=F32
@@ -36,34 +42,31 @@
     return both[:, :rank] + both[:, rank:]
 
 
-def sketch_kernel(step, block, samples_ref, start_ref, local_ref, held_ref, start, sems):
+def sketch_kernel(step, block, samples_ref, start_ref, local_ref, held_ref, start, sems, start_sem):
     rows, columns = held_ref.shape
     rank = local_ref.shape[1]
+    whole = pltpu.make_async_copy(start_ref, start, start_sem)
+    whole.start()
     copies = []
     for i in range(columns // step):
         at = pl.ds(i * step, step)
-        pair = (
-            pltpu.make_async_copy(start_ref.at[at], start.at[at], sems.at[0, i]),
-            pltpu.make_async_copy(samples_ref.at[:, at], held_ref.at[:, at], sems.at[1, i]),
-        )
-        for copy in pair:
-            copy.start()
-        copies.append(pair)
-    for i, pair in enumerate(copies):
-        for copy in pair:
-            copy.wait()
+        copies.append(pltpu.make_async_copy(samples_ref.at[:, at], held_ref.at[:, at], sems.at[i]))
+        copies[-1].start()
+    whole.wait()
+    right = jnp.concatenate(halves(start[...]), axis=1)
+    for i, copy in enumerate(copies):
+        copy.wait()
         at = slice(i * step, (i + 1) * step)
-        right = jnp.concatenate(halves(start[at]), axis=1)
         for first in range(0, rows, block):
             here = slice(first, first + block)
             left = jnp.concatenate(halves(held_ref[here, at]), axis=0)
-            both = dot(left, right, ((1,), (0,)))
+            both = dot(left, right[at], ((1,), (0,)))
             both = both[:block] + both[block:]
             both = both[:, :rank] + both[:, rank:]
             local_ref[here] = both if i == 0 else local_ref[here] + both
 
 
-def sketch_product(samples, start_basis, step=256, block=128):
+def sketch_product(samples, start_basis, step=512, block=128):
     rows, columns = samples.shape
     rank = start_basis.shape[1]
     samples, start_basis = (
@@ -79,7 +82,8 @@
         ),
         scratch_shapes=[
             pltpu.VMEM((columns, rank), F32),
-            pltpu.SemaphoreType.DMA((2, columns // step)),
+            pltpu.SemaphoreType.DMA((columns // step,)),
+            pltpu.SemaphoreType.DMA,
         ],
         compiler_params=pltpu.CompilerParams(vmem_limit_bytes=LIMIT),
         cost_estimate=cost(8 * rows * columns * rank, rows * columns, rows * rank),
@@ -117,16 +121,18 @@
         other_ref[here] = jnp.where(core == 0, for_second, for_first)
 
     sketch = sketch_ref[...]
-    gram = dot(sketch, sketch, ((0,), (0,)), HIGHEST)
+    parts = thirds(sketch)
+    both = dot(parts[0], jnp.concatenate(parts, axis=1), ((0,), (0,)))
+    mixed = both[:, rank : 2 * rank] + both[:, 2 * rank :]
+    gram = both[:, :rank] + dot(parts[1], parts[1], ((0,), (0,))) + (mixed + mixed.T)
     tiles = [gram[at : at + SUBLANES] for at in range(0, rank, SUBLANES)]
     packed = packed_tiles(tiles)
-    middle = len(packed) // 2 + 1
-    first, second = packed[:middle], packed[middle:]
-    second += [jnp.zeros_like(gram[:SUBLANES])] * (len(first) - len(second))
+    middle = len(packed) // 2
+    first, second = packed[:middle] + packed[-1:], packed[middle:]
     for i, pair in enumerate(zip(first, second)):
         give(samples_ref.shape[1] // 2 + SUBLANES * i, *pair)
 
-    high, low = halves(sketch)
+    high, low = parts[:2]
     sketch_halves[:, :rank] = high
     sketch_halves[:, rank:] = low
     for at in range(0, samples_ref.shape[1], step):
@@ -143,14 +149,18 @@
     for t in range(1, count // 2):
         start = SUBLANES * t
         packed.append(jnp.where(lane >= start, tiles[t], pltpu.roll(tiles[count - t], start, 1)))
-    return packed + [tiles[count // 2]]
+    last = tiles[count // 2]
+    lower = pltpu.roll(pltpu.roll(last, size // 2, 1), SUBLANES // 2, 0)
+    return packed + [jnp.where(lane >= size // 2, last, lower)]
 
 
 def unpacked_tiles(packed):
     count, size = 2 * (len(packed) - 1), packed[0].shape[1]
+    sub = lax.broadcasted_iota(jnp.int32, packed[0].shape, 0)
     tiles = list(packed) + [None] * (count - len(packed))
     for t in range(1, count // 2):
         tiles[count - t] = pltpu.roll(packed[t], size - SUBLANES * t, 1)
+    tiles[count // 2] = jnp.where(sub < SUBLANES // 2, packed[-1], pltpu.roll(packed[-1], size // 2, 1))
     upper = jnp.concatenate(tiles, axis=0)
     row = lax.broadcasted_iota(jnp.int32, upper.shape, 0)
     lane = lax.broadcasted_iota(jnp.int32, upper.shape, 1)
@@ -159,13 +169,13 @@
 
 
 def gram_rows(rank):
-    return SUBLANES * (rank // SUBLANES // 4 + 1)
-
-
-def products(samples, sketch, share, step=256):
+    return rank // 4 + SUBLANES // 2
+
+
+def products(samples, sketch, share, step=512):
     rows, columns = samples.shape
     rank = sketch.shape[1]
-    half = jax.ShapeDtypeStruct((columns // 2 + gram_rows(rank), rank), F32)
+    half = jax.ShapeDtypeStruct((columns // 2 + gram_rows(rank) + SUBLANES // 2, rank), F32)
     return pl.pallas_call(
         functools.partial(products_kernel, step, share),
         in_specs=[WHOLE, WHOLE],
@@ -186,8 +196,7 @@
 
 
 def spread_kernel(share, inner, outer, gram, own_ref, others_ref, out_ref):
-    rows = own_ref.shape[0]
-    theirs = (1 - lax.axis_index("core")) * rows
+    theirs = (1 - lax.axis_index("core")) * own_ref.shape[0]
 
     def total(at, count):
         there = pl.ds(pl.multiple_of(theirs + at, SUBLANES), count)
@@ -206,7 +215,7 @@
     rows, rank = own.shape
     outer = (rows - gram) // share // inner
     size = outer * share + gram
-    out = pl.pallas_call(
+    return pl.pallas_call(
         functools.partial(spread_kernel, share, inner, outer, gram),
         in_specs=[WHOLE] * 2,
         out_specs=WHOLE,
@@ -215,50 +224,57 @@
         cost_estimate=cost(rows * rank, rows * rank, inner * size * rank),
         name="spread",
     )(own, others)
-    return out.reshape(inner, size, rank)
-
-
-def respread_kernel(share, count, gram, parts_ref, out_ref):
-    parts = [parts_ref.at[i] for i in range(parts_ref.shape[0])]
-    last = added(parts, count * share, gram)
-    for i in range(count):
-        out_ref[i, :share] = added(parts, i * share, share)
-        out_ref[i, share:] = last
-
-
-def respread(parts, share, gram):
-    count = (parts.shape[1] - gram) // share
-    rank = parts.shape[2]
-    return pl.pallas_call(
-        functools.partial(respread_kernel, share, count, gram),
+
+
+def added(parts_ref, count, at, rows):
+    size = parts_ref.shape[0] // count
+    total = parts_ref[at : at + rows]
+    for i in range(1, count):
+        total = total + parts_ref[i * size + at : i * size + at + rows]
+    return total
+
+
+def respread_kernel(share, inner, outer, gram, parts_ref, out_ref):
+    last = added(parts_ref, inner, outer * share, gram)
+    for o in range(outer):
+        here = (share + gram) * o
+        out_ref[here : here + share] = added(parts_ref, inner, o * share, share)
+        out_ref[here + share : here + share + gram] = last
+
+
+def respread(parts, share, inner, outer, gram):
+    rank = parts.shape[1]
+    return pl.pallas_call(
+        functools.partial(respread_kernel, share, inner, outer, gram),
         in_specs=[WHOLE],
         out_specs=WHOLE,
-        out_shape=jax.ShapeDtypeStruct((count, share + gram, rank), F32),
+        out_shape=jax.ShapeDtypeStruct((outer * (share + gram), rank), F32),
         compiler_params=pltpu.CompilerParams(vmem_limit_bytes=LIMIT),
         cost_estimate=cost(parts.size, parts.size, parts.size),
         name="respread",
     )(parts)
 
 
-def finish_kernel(parts_ref, mine_ref, gram_ref):
-    parts = [parts_ref.at[i] for i in range(parts_ref.shape[0])]
-    share, gram = mine_ref.shape[0], gram_ref.shape[0]
-    mine_ref[...] = added(parts, 0, share)
-    gram_ref[...] = added(parts, share, gram)
-
-
-def finish(parts, share):
-    rows, rank = parts.shape[1:]
-    return pl.pallas_call(
-        finish_kernel,
+def finish_kernel(outer, gram, parts_ref, mine_ref, gram_ref):
+    share, whole = mine_ref.shape[0], gram // SUBLANES * SUBLANES
+    mine_ref[...] = added(parts_ref, outer, 0, share)
+    gram_ref[:whole] = added(parts_ref, outer, share, whole)
+    last = added(parts_ref, outer, share + whole, gram - whole)
+    gram_ref[whole:] = jnp.concatenate([last, last], axis=0)
+
+
+def finish(parts, share, outer, gram):
+    rank = parts.shape[1]
+    return pl.pallas_call(
+        functools.partial(finish_kernel, outer, gram),
         in_specs=[WHOLE],
         out_specs=(WHOLE, WHOLE),
         out_shape=(
             jax.ShapeDtypeStruct((share, rank), F32),
-            jax.ShapeDtypeStruct((rows - share, rank), F32),
+            jax.ShapeDtypeStruct((gram + SUBLANES // 2, rank), F32),
         ),
         compiler_params=pltpu.CompilerParams(vmem_limit_bytes=LIMIT),
-        cost_estimate=cost(parts.size, parts.size, rows * rank),
+        cost_estimate=cost(parts.size, parts.size, (share + gram) * rank),
         name="finish",
     )(parts)
 
@@ -272,7 +288,9 @@
     sub = lax.broadcasted_iota(jnp.int32, (SUBLANES, size), 0)
     down = lambda values, row: jnp.broadcast_to(values[row : row + 1, :], values.shape)
     across = lambda values, column: jnp.broadcast_to(values[:, column : column + 1], values.shape)
-    packed = [packed_ref[SUBLANES * i : SUBLANES * (i + 1)] for i in range(count // 2 + 1)]
+    middle = count // 4
+    packed = [packed_ref[SUBLANES * i : SUBLANES * (i + 1)] for i in range(2 * (middle + 1))]
+    packed = packed[:middle] + packed[middle + 1 :]
     tiles = [tile / total for tile in unpacked_tiles(packed)]
     columns = lambda t, j: [across(tiles[t], SUBLANES * j + k) for k in range(SUBLANES)]
     own, below = columns(0, 0), {1: columns(1, 0)}
@@ -370,9 +388,10 @@
 
     own, other = products(samples, sketch, share)
     others = lax.all_gather(other, "core", axis=0, tiled=True)
-    parts = exchange(spread(own, others, share, x, gram), "x")
-    parts = exchange(respread(parts, share, gram), "y")
-    mine, half = finish(parts, share)
+    trip = lambda parts, axis, n: exchange(parts.reshape(n, -1, 4, rank), axis).reshape(-1, rank)
+    parts = trip(spread(own, others, share, x, gram), "x", x)
+    parts = trip(respread(parts, share, x, y, gram), "y", y)
+    mine, half = finish(parts, share, y, gram)
     packed = lax.all_gather(half, "core", axis=0, tiled=True)
     return factor(packed, mine, sketch, float(total))
 

time: 84.5 us -> 83.8 us (level)
  no operation moved by 1% of the time
where the time goes in v6:
time: 83.8 us; the launch traced here: 83.5 us
  blocking collectives  74.7 us (89%)
  Pallas kernels  8.16 us (10%)
    all_to_all x4, blocking collectives, exchange(): return lax.all_to_all(parts, axis, 0, 0)  64.4 us
    all_gather x1, blocking collectives, body(): others = lax.all_gather(other, 'core', axis=0, tiled=True)  5.81 us
    all_gather x1, blocking collectives, body(): packed = lax.all_gather(half, 'core', axis=0, tiled=True)  4.52 us
    pallas_call x1, Pallas kernels, factor(): pl.pallas_call(functools.partial(factor_kernel, total), in_specs=[WHOLE]...  3.99 us
    pallas_call x1, Pallas kernels, sketch_product(): pl.pallas_call(functools.partial(sketch_kernel, step, block), in_specs=[p...  2.82 us

profile of v6, /device:TPU:1, one launch (start us, length us, event | category | flops | bytes accessed | tf_op | source)
XLA Modules:
  0.0 83.5 jit_solution(3827202155120616905)
XLA Ops:
  0.6 2.8 %sketch_product.1 = (f32[768,128]{1,0:T(8,128)S(1)}, f32[768,1024]{1,0:T(8,128)S(1)}) custom-call(f32[768,1024]{1,0:T(8,128)} %samples_ref.1, f32[1024,128]{1,0:T(8,128)} %start_ref.1), custom_call_target="tpu_custom_call" | custom-call | flops 805306368 | bytes 3538944 | tf_op jit(solution)/shard_map/sketch_product/pallas_call | solution.py:75
  3.5 24.2 %all_to_all.20.parts_ref = f32[8,96,128]{2,1,0:T(8,128)S(1)} all-to-all(f32[8,96,128]{2,1,0:T(8,128)S(1)} %bitcast.12), channel_id=1, replica_groups=mesh['y'=8,'x'=4,'core'=2,'col'=8] {'col'}, dimensions={0} | all-to-all | bytes 786432 | tf_op jit(solution)/shard_map/all_to_all | solution.py:375
  27.7 14.1 %all_to_all.21 = f32[8,96,128]{2,1,0:T(8,128)S(1)} all-to-all(f32[8,96,128]{2,1,0:T(8,128)S(1)} %sum_and_copy.1), channel_id=1, replica_groups=mesh['y'=8,'x'=4,'core'=2,'col'=8] {'col'}, dimensions={0} | all-to-all | bytes 786432 | tf_op jit(solution)/shard_map/all_to_all | solution.py:375
  41.8 1.2 %products.1 = (f32[552,128]{1,0:T(8,128)S(1)}, f32[552,128]{1,0:T(8,128)S(1)}) custom-call(f32[768,1024]{1,0:T(8,128)S(1)} %get-tuple-element.9.samples_ref, f32[768,128]{1,0:T(8,128)S(1)} %bitcast.6), custom_call_target="tpu_custom_call" | custom-call | flops 805306368 | bytes 3670016 | tf_op jit(solution)/shard_map/products/pallas_call | solution.py:179
  43.0 5.8 %all_gather.6.others_ref = f32[1104,128]{1,0:T(8,128)S(1)} all-gather(f32[552,128]{1,0:T(8,128)S(1)} %get-tuple-element.12), channel_id=1, replica_groups=mesh['y'=8,'x'=4,'core'=2,'col'=8] {'core'}, dimensions={0}, use_global_device_ids=true | all-gather | bytes 847872 | tf_op jit(solution)/shard_map/all_gather | solution.py:390
  48.9 10.7 %all_to_all.22 = f32[4,41,4,128]{3,2,1,0:T(4,128)S(1)} all-to-all(f32[4,41,4,128]{3,2,1,0:T(4,128)S(1)} %bitcast.8), channel_id=1, replica_groups=mesh['y'=8,'x'=4,'core'=2,'col'=8] {'x'}, dimensions={0} | all-to-all | bytes 671744 | tf_op jit(solution)/shard_map/all_to_all | solution.py:375
  59.6 15.4 %all_to_all.23 = f32[8,13,4,128]{3,2,1,0:T(4,128)S(1)} all-to-all(f32[8,13,4,128]{3,2,1,0:T(4,128)S(1)} %bitcast.10), channel_id=1, replica_groups=mesh['y'=8,'x'=4,'core'=2,'col'=8] {'y'}, dimensions={0} | all-to-all | bytes 425984 | tf_op jit(solution)/shard_map/all_to_all | solution.py:375
  75.0 4.5 %all_gather.7.packed_ref = f32[80,128]{1,0:T(8,128)S(1)} all-gather(f32[40,128]{1,0:T(8,128)S(1)} %get-tuple-element.13), channel_id=1, replica_groups=mesh['y'=8,'x'=4,'core'=2,'col'=8] {'core'}, dimensions={0}, use_global_device_ids=true | all-gather | bytes 61440 | tf_op jit(solution)/shard_map/all_gather | solution.py:395
  79.5 4.0 %factor.1 = (f32[768,128]{1,0:T(8,128)}, f32[128,128]{1,0:T(8,128)}, f32[1,16,128]{2,1,0:T(8,128)}) custom-call(f32[80,128]{1,0:T(8,128)S(1)} %all_gather.7.packed_ref, f32[16,128]{1,0:T(8,128)S(1)} %get-tuple-element.14.mine_ref, f32[768,128]{1,0:T(8,128)S(1)} %bitcast.7), custom_call_target="tpu_custom_call" | custom-call | flops 1258291200 | bytes 786432 | tf_op jit(solution)/shard_map/factor/pallas_call | solution.py:358
  (4 shorter events, 0.1 us)

commit v7 on v6

--- a/solution.py
+++ b/solution.py
@@ -298,7 +298,7 @@
         base = SUBLANES * j
         here = slice(base, base + SUBLANES)
         inside = (lane >= base) & (lane < base + SUBLANES)
-        near = range(j + 1, min(j + 1 + 4, count))
+        near = range(j + 1, min(j + 1 + 3, count))
         for t in near[1:]:
             below[t] = columns(t, j)
         ahead = [columns(t, j + 1) for t in near[:2]]

time: 83.8 us -> 83.8 us (level)
  no operation moved by 1% of the time
where the time goes in v7:
time: 83.8 us; the launch traced here: 83.5 us
  blocking collectives  74.7 us (89%)
  Pallas kernels  8.16 us (10%)
    all_to_all x4, blocking collectives, exchange(): return lax.all_to_all(parts, axis, 0, 0)  64.4 us
    all_gather x1, blocking collectives, body(): others = lax.all_gather(other, 'core', axis=0, tiled=True)  5.81 us
    all_gather x1, blocking collectives, body(): packed = lax.all_gather(half, 'core', axis=0, tiled=True)  4.52 us
    pallas_call x1, Pallas kernels, factor(): pl.pallas_call(functools.partial(factor_kernel, total), in_specs=[WHOLE]...  3.99 us
    pallas_call x1, Pallas kernels, sketch_product(): pl.pallas_call(functools.partial(sketch_kernel, step, block), in_specs=[p...  2.82 us

profile of v7, /device:TPU:1, one launch (start us, length us, event | category | flops | bytes accessed | tf_op | source)
XLA Modules:
  0.0 83.5 jit_solution(3602996222114516202)
XLA Ops:
  0.6 2.8 %sketch_product.1 = (f32[768,128]{1,0:T(8,128)S(1)}, f32[768,1024]{1,0:T(8,128)S(1)}) custom-call(f32[768,1024]{1,0:T(8,128)} %samples_ref.1, f32[1024,128]{1,0:T(8,128)} %start_ref.1), custom_call_target="tpu_custom_call" | custom-call | flops 805306368 | bytes 3538944 | tf_op jit(solution)/shard_map/sketch_product/pallas_call | solution.py:75
  3.5 24.2 %all_to_all.20.parts_ref = f32[8,96,128]{2,1,0:T(8,128)S(1)} all-to-all(f32[8,96,128]{2,1,0:T(8,128)S(1)} %bitcast.12), channel_id=1, replica_groups=mesh['y'=8,'x'=4,'core'=2,'col'=8] {'col'}, dimensions={0} | all-to-all | bytes 786432 | tf_op jit(solution)/shard_map/all_to_all | solution.py:375
  27.7 14.1 %all_to_all.21 = f32[8,96,128]{2,1,0:T(8,128)S(1)} all-to-all(f32[8,96,128]{2,1,0:T(8,128)S(1)} %sum_and_copy.1), channel_id=1, replica_groups=mesh['y'=8,'x'=4,'core'=2,'col'=8] {'col'}, dimensions={0} | all-to-all | bytes 786432 | tf_op jit(solution)/shard_map/all_to_all | solution.py:375
  41.8 1.2 %products.1 = (f32[552,128]{1,0:T(8,128)S(1)}, f32[552,128]{1,0:T(8,128)S(1)}) custom-call(f32[768,1024]{1,0:T(8,128)S(1)} %get-tuple-element.9.samples_ref, f32[768,128]{1,0:T(8,128)S(1)} %bitcast.6), custom_call_target="tpu_custom_call" | custom-call | flops 805306368 | bytes 3670016 | tf_op jit(solution)/shard_map/products/pallas_call | solution.py:179
  43.0 5.8 %all_gather.6.others_ref = f32[1104,128]{1,0:T(8,128)S(1)} all-gather(f32[552,128]{1,0:T(8,128)S(1)} %get-tuple-element.12), channel_id=1, replica_groups=mesh['y'=8,'x'=4,'core'=2,'col'=8] {'core'}, dimensions={0}, use_global_device_ids=true | all-gather | bytes 847872 | tf_op jit(solution)/shard_map/all_gather | solution.py:390
  48.9 10.7 %all_to_all.22 = f32[4,41,4,128]{3,2,1,0:T(4,128)S(1)} all-to-all(f32[4,41,4,128]{3,2,1,0:T(4,128)S(1)} %bitcast.8), channel_id=1, replica_groups=mesh['y'=8,'x'=4,'core'=2,'col'=8] {'x'}, dimensions={0} | all-to-all | bytes 671744 | tf_op jit(solution)/shard_map/all_to_all | solution.py:375
  59.6 15.4 %all_to_all.23 = f32[8,13,4,128]{3,2,1,0:T(4,128)S(1)} all-to-all(f32[8,13,4,128]{3,2,1,0:T(4,128)S(1)} %bitcast.10), channel_id=1, replica_groups=mesh['y'=8,'x'=4,'core'=2,'col'=8] {'y'}, dimensions={0} | all-to-all | bytes 425984 | tf_op jit(solution)/shard_map/all_to_all | solution.py:375
  75.0 4.5 %all_gather.7.packed_ref = f32[80,128]{1,0:T(8,128)S(1)} all-gather(f32[40,128]{1,0:T(8,128)S(1)} %get-tuple-element.13), channel_id=1, replica_groups=mesh['y'=8,'x'=4,'core'=2,'col'=8] {'core'}, dimensions={0}, use_global_device_ids=true | all-gather | bytes 61440 | tf_op jit(solution)/shard_map/all_gather | solution.py:395
  79.5 4.0 %factor.1 = (f32[768,128]{1,0:T(8,128)}, f32[128,128]{1,0:T(8,128)}, f32[1,16,128]{2,1,0:T(8,128)}) custom-call(f32[80,128]{1,0:T(8,128)S(1)} %all_gather.7.packed_ref, f32[16,128]{1,0:T(8,128)S(1)} %get-tuple-element.14.mine_ref, f32[768,128]{1,0:T(8,128)S(1)} %bitcast.7), custom_call_target="tpu_custom_call" | custom-call | flops 1258291200 | bytes 786432 | tf_op jit(solution)/shard_map/factor/pallas_call | solution.py:358
  (4 shorter events, 0.1 us)

commit v8 on v7

--- a/solution.py
+++ b/solution.py
@@ -280,7 +280,7 @@
 
 
 def factor_kernel(
-    total, packed_ref, mine_ref, sketch_ref, basis_ref, upper_ref, projected_ref, inverse_ref
+    total, packed_ref, mine_ref, sketch_ref, basis_ref, upper_ref, projected_ref, inverse_ref, pieces_ref
 ):
     size = upper_ref.shape[0]
     count = size // SUBLANES
@@ -292,6 +292,8 @@
     packed = [packed_ref[SUBLANES * i : SUBLANES * (i + 1)] for i in range(2 * (middle + 1))]
     packed = packed[:middle] + packed[middle + 1 :]
     tiles = [tile / total for tile in unpacked_tiles(packed)]
+    first, second, third = thirds(sketch_ref[...])
+    pieces_ref[...] = jnp.concatenate([second, first, third], axis=1)
     columns = lambda t, j: [across(tiles[t], SUBLANES * j + k) for k in range(SUBLANES)]
     own, below = columns(0, 0), {1: columns(1, 0)}
     for j in range(count):
@@ -349,7 +351,11 @@
         block = jnp.where(lane - base >= sub, block, 0.0)
         upper_ref[here, :] = jnp.where(lane >= base + SUBLANES, done, block)
         inverse_ref[here, :] = jnp.where(lane < base + SUBLANES, done, 0.0)
-    basis_ref[...] = dot(sketch_ref[...], inverse_ref[...], ((1,), (1,)), HIGHEST)
+    first, second, third = thirds(inverse_ref[...])
+    right = jnp.concatenate([jnp.concatenate([part] * 2, axis=1) for part in (first, second)], axis=0)
+    both = dot(pieces_ref[:, : 2 * size], right, ((1,), (1,)))
+    rest = dot(pieces_ref[:, size:], jnp.concatenate([third, first], axis=1), ((1,), (1,)))
+    basis_ref[...] = both[:, :size] + (both[:, size:] + rest)
     projected_ref[0] = dot(mine_ref[...], inverse_ref[...], ((1,), (1,)), HIGHEST) * (1.0 / total**0.5)
 
 
@@ -364,7 +370,7 @@
             jax.ShapeDtypeStruct((rank, rank), F32),
             jax.ShapeDtypeStruct((1,) + mine.shape, F32),
         ),
-        scratch_shapes=[pltpu.VMEM((rank, rank), F32)],
+        scratch_shapes=[pltpu.VMEM((rank, rank), F32), pltpu.VMEM((rows, 3 * rank), BF16)],
         compiler_params=pltpu.CompilerParams(vmem_limit_bytes=LIMIT),
         cost_estimate=cost(50 * 2 * rows * rank * rank, rows * rank, rows * rank),
         name="factor",

time: 83.8 us -> 83.7 us (level)
  no operation moved by 1% of the time
where the time goes in v8:
time: 83.7 us; the launch traced here: 83.4 us
  blocking collectives  74.7 us (89%)
  Pallas kernels  8.04 us (10%)
    all_to_all x4, blocking collectives, exchange(): return lax.all_to_all(parts, axis, 0, 0)  64.4 us
    all_gather x1, blocking collectives, body(): others = lax.all_gather(other, 'core', axis=0, tiled=True)  5.81 us
    all_gather x1, blocking collectives, body(): packed = lax.all_gather(half, 'core', axis=0, tiled=True)  4.52 us
    pallas_call x1, Pallas kernels, factor(): pl.pallas_call(functools.partial(factor_kernel, total), in_specs=[WHOLE]...  3.86 us
    pallas_call x1, Pallas kernels, sketch_product(): pl.pallas_call(functools.partial(sketch_kernel, step, block), in_specs=[p...  2.82 us

profile of v8, /device:TPU:1, one launch (start us, length us, event | category | flops | bytes accessed | tf_op | source)
XLA Modules:
  0.0 83.4 jit_solution(14878834236093274333)
XLA Ops:
  0.6 2.8 %sketch_product.1 = (f32[768,128]{1,0:T(8,128)S(1)}, f32[768,1024]{1,0:T(8,128)S(1)}) custom-call(f32[768,1024]{1,0:T(8,128)} %samples_ref.1, f32[1024,128]{1,0:T(8,128)} %start_ref.1), custom_call_target="tpu_custom_call" | custom-call | flops 805306368 | bytes 3538944 | tf_op jit(solution)/shard_map/sketch_product/pallas_call | solution.py:75
  3.5 24.2 %all_to_all.20.parts_ref = f32[8,96,128]{2,1,0:T(8,128)S(1)} all-to-all(f32[8,96,128]{2,1,0:T(8,128)S(1)} %bitcast.12), channel_id=1, replica_groups=mesh['y'=8,'x'=4,'core'=2,'col'=8] {'col'}, dimensions={0} | all-to-all | bytes 786432 | tf_op jit(solution)/shard_map/all_to_all | solution.py:381
  27.7 14.1 %all_to_all.21 = f32[8,96,128]{2,1,0:T(8,128)S(1)} all-to-all(f32[8,96,128]{2,1,0:T(8,128)S(1)} %sum_and_copy.1), channel_id=1, replica_groups=mesh['y'=8,'x'=4,'core'=2,'col'=8] {'col'}, dimensions={0} | all-to-all | bytes 786432 | tf_op jit(solution)/shard_map/all_to_all | solution.py:381
  41.8 1.2 %products.1 = (f32[552,128]{1,0:T(8,128)S(1)}, f32[552,128]{1,0:T(8,128)S(1)}) custom-call(f32[768,1024]{1,0:T(8,128)S(1)} %get-tuple-element.9.samples_ref, f32[768,128]{1,0:T(8,128)S(1)} %bitcast.6), custom_call_target="tpu_custom_call" | custom-call | flops 805306368 | bytes 3670016 | tf_op jit(solution)/shard_map/products/pallas_call | solution.py:179
  43.0 5.8 %all_gather.6.others_ref = f32[1104,128]{1,0:T(8,128)S(1)} all-gather(f32[552,128]{1,0:T(8,128)S(1)} %get-tuple-element.12), channel_id=1, replica_groups=mesh['y'=8,'x'=4,'core'=2,'col'=8] {'core'}, dimensions={0}, use_global_device_ids=true | all-gather | bytes 847872 | tf_op jit(solution)/shard_map/all_gather | solution.py:396
  48.9 10.7 %all_to_all.22 = f32[4,41,4,128]{3,2,1,0:T(4,128)S(1)} all-to-all(f32[4,41,4,128]{3,2,1,0:T(4,128)S(1)} %bitcast.8), channel_id=1, replica_groups=mesh['y'=8,'x'=4,'core'=2,'col'=8] {'x'}, dimensions={0} | all-to-all | bytes 671744 | tf_op jit(solution)/shard_map/all_to_all | solution.py:381
  59.6 15.4 %all_to_all.23 = f32[8,13,4,128]{3,2,1,0:T(4,128)S(1)} all-to-all(f32[8,13,4,128]{3,2,1,0:T(4,128)S(1)} %bitcast.10), channel_id=1, replica_groups=mesh['y'=8,'x'=4,'core'=2,'col'=8] {'y'}, dimensions={0} | all-to-all | bytes 425984 | tf_op jit(solution)/shard_map/all_to_all | solution.py:381
  75.0 4.5 %all_gather.7.packed_ref = f32[80,128]{1,0:T(8,128)S(1)} all-gather(f32[40,128]{1,0:T(8,128)S(1)} %get-tuple-element.13), channel_id=1, replica_groups=mesh['y'=8,'x'=4,'core'=2,'col'=8] {'core'}, dimensions={0}, use_global_device_ids=true | all-gather | bytes 61440 | tf_op jit(solution)/shard_map/all_gather | solution.py:401
  79.5 3.9 %factor.1 = (f32[768,128]{1,0:T(8,128)}, f32[128,128]{1,0:T(8,128)}, f32[1,16,128]{2,1,0:T(8,128)}) custom-call(f32[80,128]{1,0:T(8,128)S(1)} %all_gather.7.packed_ref, f32[16,128]{1,0:T(8,128)S(1)} %get-tuple-element.14.mine_ref, f32[768,128]{1,0:T(8,128)S(1)} %bitcast.7), custom_call_target="tpu_custom_call" | custom-call | flops 1258291200 | bytes 786432 | tf_op jit(solution)/shard_map/factor/pallas_call | solution.py:364
  (4 shorter events, 0.1 us)
